TPU v7x, 512 devices: a whole 4x4x16 slice. The times are simulated.
512 devices in a mesh: branch: 16 (over z_lo, y), shard: 32 (over z_hi, x, core).
Axes of the slice: x: 4, y: 4, z: 16 (z_hi: 4, z_lo: 4; z = z_hi * 4 + z_lo), core: 2. Of those that a mesh axis runs over, the one named last changes fastest.
Arguments:
- tokens: bfloat16 [2048, 4096], P('branch', 'shard'), may hold values from -45 to 45
- context: bfloat16 [2048, 2048], P('branch', 'shard'), may hold values from -6 to 6
- attn_weights: bfloat16 [16, 2048, 4096], P('branch', None, 'shard'), may hold values from -0.125 to 0.125
- norm_gain: bfloat16 [4096], P('shard'), may hold values from 0.099609375 to 1.8984375
- router: bfloat16 [4096, 16], P('shard'), may hold values from -0.375 to 0.375
- routes: int32 [2048, 2], P('branch'), may hold values from 0 to 15, all different within a row; in each aligned block of 128 rows (0 to 127, 128 to 255, ...) at most 24 rows name the same one
- gate_w: bfloat16 [16, 4096, 5632], P('branch', 'shard'), may hold values from -0.09375 to 0.09375
- up_w: bfloat16 [16, 4096, 5632], P('branch', 'shard'), may hold values from -0.09375 to 0.09375
- down_w: bfloat16 [16, 5632, 4096], P('branch', None, 'shard'), may hold values from -0.15625 to 0.15625
Outputs:
- attended: bfloat16 [2048, 4096], P('branch', 'shard')
- mixed: bfloat16 [2048, 4096], P('branch', 'shard')
Inputs may be any that keep to these rules, and one draw needn't show every extreme that they name: `routes`: the two experts of a token differ; within each aligned block of 128 tokens (one group) no expert is named by more than 24 tokens, a bound that some block reaches.
All inputs are finite; a program needn't handle non-finite values.
Results may differ from a plain program's by a relative error of at most 0.03.
Values may be sent and summed in bfloat16 or wider, within the bound.
No kernel may reach another device: no remote copies, remote signals or barrier semaphores. Data moves between devices by JAX's collectives and lax.ppermute only.
A program may use at most 64 MiB of HBM per device.

v0:
```python
import jax
import jax.numpy as jnp
from jax import lax
from jax.sharding import PartitionSpec as P

D = 4096


def group_slots(group_routes, experts):
    flat = group_routes.reshape(-1)
    onehot = (flat[:, None] == jnp.arange(experts, dtype=jnp.int32)[None, :]).astype(jnp.int32)
    before = jnp.cumsum(onehot, axis=0) - onehot
    return jnp.sum(before * onehot, axis=1).reshape(group_routes.shape)


def body(tokens, context, attn_weights, norm_gain, router, routes, gate_w, up_w, down_w):
    experts = router.shape[1]
    token_count = tokens.shape[0]
    local_width = tokens.shape[1]
    capacity = 3 * token_count // experts
    summed = lax.psum(attn_weights[0].astype(jnp.float32).astype(jnp.bfloat16), "branch").astype(
        jnp.float32
    )
    merged = (summed / experts).astype(jnp.bfloat16)
    attention_out = jnp.dot(
        lax.all_gather(context, "shard", axis=1, tiled=True),
        merged,
        preferred_element_type=jnp.float32,
    )
    attended_f = tokens.astype(jnp.float32) + attention_out
    gain = norm_gain.astype(jnp.float32)[None, :]
    squares = jnp.sum(attended_f * attended_f, axis=1)
    router_f = router.astype(jnp.float32)
    square_sum = lax.psum(squares, "shard")
    scale = lax.rsqrt(square_sum / D + 1e-05)[:, None]
    normed_f = attended_f * scale * gain
    logits = lax.psum(jnp.dot(normed_f, router_f, precision=lax.Precision.HIGHEST), "shard")
    normed = normed_f.astype(jnp.bfloat16)
    weights = jax.nn.sigmoid(jnp.take_along_axis(logits, routes, axis=1))
    slots = group_slots(routes, experts)
    places = routes * capacity + slots
    table = jnp.any(
        jnp.arange(experts * capacity, dtype=jnp.int32)[:, None, None] == places[None, :, :], axis=2
    )
    outgoing = jnp.dot(
        table.astype(jnp.bfloat16), normed, preferred_element_type=jnp.float32
    ).astype(jnp.bfloat16)
    gate_rel, up_rel = (
        lax.all_to_all(gate_w[0], "shard", split_axis=1, concat_axis=0, tiled=True),
        lax.all_to_all(up_w[0], "shard", split_axis=1, concat_axis=0, tiled=True),
    )
    received = lax.all_to_all(outgoing, "branch", split_axis=0, concat_axis=0, tiled=True)
    piece = lax.all_gather(received, "shard", axis=1, tiled=True)
    gate = jnp.dot(piece, gate_rel, preferred_element_type=jnp.float32)
    up = jnp.dot(piece, up_rel, preferred_element_type=jnp.float32)
    hidden = (jax.nn.silu(gate) * up).astype(jnp.bfloat16)
    down_rel = lax.all_to_all(down_w[0], "shard", split_axis=0, concat_axis=1, tiled=True)
    expert_out = lax.psum_scatter(
        lax.dot_general(
            down_rel, hidden, (((0,), (1,)), ((), ())), preferred_element_type=jnp.float32
        ).astype(jnp.bfloat16),
        "shard",
        scatter_dimension=0,
        tiled=True,
    )
    returned = lax.all_to_all(expert_out, "branch", split_axis=1, concat_axis=1, tiled=True)
    picked = jnp.take(returned, places.reshape(-1), axis=1).reshape(local_width, token_count, 2)
    mixed = jnp.einsum("dtk,tk->td", picked.astype(jnp.float32), weights)
    return (attended_f.astype(jnp.bfloat16), mixed.astype(jnp.bfloat16))


def solution(mesh):
    in_specs = (
        P("branch", "shard"),
        P("branch", "shard"),
        P("branch", None, "shard"),
        P("shard"),
        P("shard", None),
        P("branch", None),
        P("branch", "shard", None),
        P("branch", "shard", None),
        P("branch", None, "shard"),
    )
    out_specs = (P("branch", "shard"), P("branch", "shard"))
    return jax.shard_map(body, mesh=mesh, in_specs=in_specs, out_specs=out_specs, check_vma=False)
```

profile of v0, /device:TPU:1, one launch (start us, length us, event | category | flops | bytes accessed | tf_op | source)
XLA Modules:
  0.0 802.0 jit_solution(6327902724145400381)
XLA Ops:
  7.9 0.9 copy.68
  12.5 62.1 %all_gather.6 = bf16[128,2048]{0,1:T(8,128)(2,1)S(1)} all-gather(bf16[128,64]{0,1:T(8,128)(2,1)} %param.10), channel_id=1, replica_groups=mesh['branch'=16,'shard'=32] {'shard'}, dimensions={1}, use_global_device_ids=true | all-gather | bytes 540672 | tf_op jit(solution)/shard_map/all_gather | solution.py:26
  74.6 103.1 %all-reduce.2.cloned.1.call-done = bf16[2048,128]{1,0:T(8,128)(2,1)} async-done(((bf16[2048,128]{1,0:T(8,128)(2,1)}), bf16[2048,128]{1,0:T(8,128)(2,1)}) %all-reduce.2.cloned.1.call-update) | async-done | bytes 524304 | tf_op jit(solution)/shard_map/psum | solution.py:21
  177.7 1.4 multiply_reduce_fusion
  179.0 94.5 %psum.22 = f32[128]{0:T(128)S(1)} all-reduce(f32[128]{0:T(128)S(1)} %get-tuple-element.14), channel_id=1, replica_groups=mesh['branch'=16,'shard'=32] {'shard'}, use_global_device_ids=true, to_apply=%region_6.7 | all-reduce | flops 128 | bytes 1024 | tf_op jit(solution)/shard_map/psum | solution.py:34
  273.5 0.9 convolution_convert_fusion.1
  274.4 6.2 all-to-all-start
  280.7 0.9 copy.73
  281.6 6.6 all-to-all-done
  288.2 81.9 %all_to_all.81 = bf16[128,32,176]{0,2,1:T(8,128)(2,1)} all-to-all(bf16[128,32,176]{0,2,1:T(8,128)(2,1)S(1)} %bitcast.83), channel_id=1, replica_groups=mesh['branch'=16,'shard'=32] {'shard'}, dimensions={1} | all-to-all | bytes 2883584 | tf_op jit(solution)/shard_map/all_to_all | solution.py:49
  370.1 7.9 all-to-all-start.3
  378.7 1.6 copy.75
  380.3 72.1 %all-to-all-done.3 = bf16[32,176,128]{2,1,0:T(8,128)(2,1)S(1)} async-done(((bf16[32,176,128]{2,1,0:T(8,128)(2,1)}), bf16[32,176,128]{2,1,0:T(8,128)(2,1)S(1)}, u32[]{:S(2)}, u32[]{:S(2)}) %all-to-all-start.3) | async-done | bytes 1441824 | tf_op jit(solution)/shard_map/all_to_all | solution.py:57
  452.4 1.1 copy-done.3
  453.5 8.0 all-to-all-start.2
  461.6 85.5 %all-gather.2.cloned.1.call-done = bf16[384,4096]{1,0:T(8,128)(2,1)} async-done(((bf16[384,128]{1,0:T(8,128)(2,1)}), bf16[384,4096]{1,0:T(8,128)(2,1)}) %all-gather.2.cloned.1.call-update) | async-done | bytes 3145744 | tf_op jit(solution)/shard_map/all_gather | solution.py:53
  547.1 3.1 fusion.6
  550.2 5.2 fusion
  555.4 2.8 copy.84
  560.2 138.4 %reduce-scatter.4.cloned.1.call-done = bf16[128,384]{1,0:T(8,128)(2,1)} async-done(((bf16[4096,384]{1,0:T(8,128)(2,1)}), bf16[128,384]{1,0:T(8,128)(2,1)}) %reduce-scatter.4.cloned.1.call-update) | async-done | bytes 98320
  698.5 1.6 copy.85
  700.2 4.3 all-to-all-start.4
  704.7 86.6 %psum.23 = f32[128,16]{0,1:T(8,128)S(1)} all-reduce(f32[128,16]{0,1:T(8,128)S(1)} %fusion.27), channel_id=1, replica_groups=mesh['branch'=16,'shard'=32] {'shard'}, use_global_device_ids=true, to_apply=%region_8.9 | all-reduce | flops 2048 | bytes 16384 | tf_op jit(solution)/shard_map/psum | solution.py:37
  791.3 2.0 gather_fusion.1
  (53 shorter events, 9.5 us)
Async XLA Ops:
  7.2 697.3 %copy-start = (bf16[128,16]{0,1:T(8,128)(2,1)S(1)}, bf16[128,16]{0,1:T(8,128)(2,1)}, u32[]{:S(2)}) copy-start(bf16[128,16]{0,1:T(8,128)(2,1)} %param.13) | copy-start | bytes 12292
  7.2 170.5 %all-reduce.2.cloned.1.call-start = ((), (), s32[]{:S(2)}) async-start(), calls=%async_computation.6 | async-start | bytes 1048576 | tf_op jit(solution)/shard_map/psum | solution.py:21
  7.9 272.7 %copy-start.1 = (bf16[1,128,5632]{2,1,0:T(8,128)(2,1)S(1)}, bf16[1,128,5632]{2,1,0:T(8,128)(2,1)}, u32[]{:S(2)}) copy-start(bf16[1,128,5632]{2,1,0:T(8,128)(2,1)} %param.15) | copy-start | bytes 4325380
  274.4 13.7 %all-to-all-start = ((bf16[16,24,128]{2,1,0:T(8,128)(2,1)}), bf16[16,24,128]{2,1,0:T(8,128)(2,1)S(1)}, u32[]{:S(2)}, u32[]{:S(2)}) async-start(bf16[16,24,128]{2,1,0:T(8,128)(2,1)} %bitcast.3), calls=%async_computation | async-start | bytes 196608 | tf_op jit(solution)/shard_map/all_to_all | solution.py:52
  288.2 81.9 %copy-start.5 = (bf16[16,24,128]{2,1,0:T(8,128)(2,1)}, bf16[16,24,128]{2,1,0:T(8,128)(2,1)S(1)}, u32[]{:S(2)}) copy-start(bf16[16,24,128]{2,1,0:T(8,128)(2,1)S(1)} %all-to-all-done) | copy-start | bytes 294916
  370.1 8.6 %copy-start.2 = (bf16[1,128,5632]{2,1,0:T(8,128)(2,1)S(1)}, bf16[1,128,5632]{2,1,0:T(8,128)(2,1)}, u32[]{:S(2)}) copy-start(bf16[1,128,5632]{2,1,0:T(8,128)(2,1)} %param.16) | copy-start | bytes 4325380
  370.1 82.3 %all-to-all-start.3 = ((bf16[32,176,128]{2,1,0:T(8,128)(2,1)}), bf16[32,176,128]{2,1,0:T(8,128)(2,1)S(1)}, u32[]{:S(2)}, u32[]{:S(2)}) async-start(bf16[32,176,128]{2,1,0:T(8,128)(2,1)} %bitcast.9), calls=%async_computation.3 | async-start | bytes 2883584 | tf_op jit(solution)/shard_map/all_to_all | solution.py:57
  378.0 169.1 %all-gather.2.cloned.1.call-start = ((), (), s32[]{:S(2)}) async-start(), calls=%async_computation.7 | async-start | bytes 3244032 | tf_op jit(solution)/shard_map/all_gather | solution.py:53
  452.4 1.1 copy-start.3
  452.4 94.7 %copy-start.4 = (bf16[128,32,176]{0,2,1:T(8,128)(2,1)S(1)}, bf16[128,32,176]{0,2,1:T(8,128)(2,1)}, u32[]{:S(2)}) copy-start(bf16[128,32,176]{0,2,1:T(8,128)(2,1)} %all_to_all.81) | copy-start | bytes 4325380
  453.5 96.6 %all-to-all-start.2 = ((bf16[128,32,176]{0,2,1:T(8,128)(2,1)}), bf16[128,32,176]{0,2,1:T(8,128)(2,1)}, u32[]{:S(2)}, u32[]{:S(2)}) async-start(bf16[128,32,176]{0,2,1:T(8,128)(2,1)} %bitcast.7), calls=%async_computation.2 | async-start | bytes 2883584 | tf_op jit(solution)/shard_map/all_to_all | solution.py:50
  461.5 237.0 %reduce-scatter.4.cloned.1.call-start = ((), (), s32[]{:S(2)}) async-start(), calls=%async_computation.8 | async-start | bytes 3244032
  558.2 0.7 copy-start.6
  700.2 93.5 %all-to-all-start.4 = ((bf16[128,16,24]{0,2,1:T(8,128)(2,1)}), bf16[128,16,24]{0,2,1:T(8,128)(2,1)S(1)}, u32[]{:S(2)}, u32[]{:S(2)}) async-start(bf16[128,16,24]{0,2,1:T(8,128)(2,1)} %bitcast.12), calls=%async_computation.4 | async-start | bytes 196608 | tf_op jit(solution)/shard_map/all_to_all | solution.py:66
Sparse Core Ops, SparseCore 0:
  10.9 166.6 all-reduce.1
  382.3 164.7 all-gather.1
  558.4 140.1 reduce-scatter.3
where the time goes:
time: 805 us; the launch traced here: 802 us
  waiting for transfers between devices  407 us (51%)
  blocking collectives  325 us (40%)
  starting transfers between devices  26.5 us (3%)
  local copies, waits for them, and re-layouts  15.6 us (2%)
  between operations  14 us (2%)
  matrix products  11.1 us (1%)
    unnamed x4, waiting for transfers between devices  140 us
    psum x1, waiting for transfers between devices, body(): lax.psum(attn_weights[0].astype(jnp.float32).astype(jnp.bfloat16), 'branch')  103 us
    psum x1, blocking collectives, body(): square_sum = lax.psum(squares, 'shard')  94.5 us
    psum x1, blocking collectives, body(): lax.psum(jnp.dot(normed_f, router_f, precision=lax.Precision.HIGHEST), 's...  86.6 us
    all_gather x1, waiting for transfers between devices, body(): piece = lax.all_gather(received, 'shard', axis=1, tiled=True)  85.5 us
    all_to_all x1, blocking collectives, body(): lax.all_to_all(gate_w[0], 'shard', split_axis=1, concat_axis=0, tiled=True)  81.9 us
    all_to_all x1, waiting for transfers between devices, body(): lax.all_to_all(down_w[0], 'shard', split_axis=0, concat_axis=1, tiled=True)  72.1 us
    all_gather x1, blocking collectives, body(): lax.all_gather(context, 'shard', axis=1, tiled=True)  62.1 us
  transfers between devices with their start and end apart: 7, of which 5 were waited for; matrix products, arithmetic and copies ran while one was open for 2% of the time, Pallas kernels for 0%

commit v1 on v0

v1 whole, which is shorter than its diff:
```python
import jax
import jax.numpy as jnp
from jax import lax
from jax.sharding import Mesh
from jax.sharding import PartitionSpec as P

D = 4096
BRANCH = ("zl", "y")
NEAR = ("x", "c")
BF = jnp.bfloat16
F32 = jnp.float32


def swap(values, axes):
    return lax.all_to_all(values, axes, split_axis=0, concat_axis=0, tiled=False)


def spread(values, axes, count):
    return swap(jnp.broadcast_to(values[None], (count,) + values.shape), axes)


def halves(values):
    high = lax.reduce_precision(values, exponent_bits=8, mantissa_bits=7)
    return high.astype(BF), (values - high).astype(BF)


def group_slots(group_routes, experts):
    flat = group_routes.reshape(-1)
    onehot = (flat[:, None] == jnp.arange(experts, dtype=jnp.int32)[None, :]).astype(jnp.int32)
    before = jnp.cumsum(onehot, axis=0) - onehot
    return jnp.sum(before * onehot, axis=1).reshape(group_routes.shape)


def body(tokens, context, attn_weights, norm_gain, router, routes, gate_w, up_w, down_w):
    experts = router.shape[1]
    token_count, width = tokens.shape
    capacity = 3 * token_count // experts
    rows = experts * capacity
    heads = attn_weights.shape[1]
    hidden_units = down_w.shape[1]
    near_units = hidden_units // 8
    own_units = near_units // 4

    gate_r = swap(gate_w[0].T.reshape(8, near_units, width), NEAR)
    up_r = swap(up_w[0].T.reshape(8, near_units, width), NEAR)
    down_r = swap(down_w[0].reshape(8, near_units, width), NEAR)

    parts = swap(attn_weights[0].reshape(experts, heads // experts, width), BRANCH)
    chunk = (jnp.sum(parts.astype(F32), axis=0) / experts).astype(BF)
    merged = spread(chunk, BRANCH, experts).reshape(heads, width)

    ctx = spread(context.T, "zh", 4)
    ctx = lax.all_gather(ctx, NEAR, axis=1, tiled=False).reshape(heads, token_count)
    attention_out = lax.dot_general(ctx, merged, (((0,), (0,)), ((), ())), preferred_element_type=F32)
    attended_f = tokens.astype(F32) + attention_out
    gained_f = attended_f * norm_gain.astype(F32)[None, :]
    squares = jnp.sum(attended_f * attended_f, axis=1, keepdims=True)
    scores = jnp.dot(gained_f, router.astype(F32), precision=lax.Precision.HIGHEST)

    places = routes * capacity + group_slots(routes, experts)
    table = jnp.any(
        jnp.arange(rows, dtype=jnp.int32)[:, None, None] == places[None, :, :], axis=2
    ).astype(BF)
    sent = jnp.dot(table, gained_f.astype(BF), preferred_element_type=F32).astype(BF)
    high, low = halves(jnp.concatenate([squares, scores], axis=1))
    extra = jnp.dot(table, jnp.concatenate([high, low], axis=1), preferred_element_type=F32)
    extra = extra.reshape(experts, capacity, 2, 1 + experts)
    own = jnp.eye(experts, dtype=F32)[:, None, None, :]
    score_part = jnp.sum(extra[..., 1:] * own, axis=3)
    extra = jnp.concatenate([extra[..., 0], score_part], axis=2).transpose(0, 2, 1).astype(BF)
    extra = jnp.pad(extra, ((0, 0), (0, 4), (0, width - capacity)))
    sent = jnp.concatenate([sent.reshape(experts, capacity, width), extra], axis=1)
    received = swap(sent, BRANCH)
    near = lax.all_gather(received, NEAR, axis=0, tiled=False)
    piece = near[:, :, :capacity].reshape(8, rows, width)
    extra = jnp.sum(near[:, :, capacity : capacity + 4, :capacity].astype(F32), axis=0)
    extra = extra.transpose(1, 0, 2).reshape(4, rows)
    extra_high, extra_low = halves(jnp.stack([extra[0] + extra[1], extra[2] + extra[3]]))
    extra = jnp.concatenate([extra_high, extra_low, jnp.zeros((12, rows), BF)])

    product = (((0, 2), (0, 2)), ((), ()))
    gate = lax.dot_general(gate_r, piece, product, preferred_element_type=F32).astype(BF)
    up = lax.dot_general(up_r, piece, product, preferred_element_type=F32).astype(BF)
    partial = jnp.concatenate(
        [
            gate.reshape(4, own_units, rows),
            up.reshape(4, own_units, rows),
            jnp.broadcast_to(extra[None], (4, 16, rows)),
        ],
        axis=1,
    )
    total = jnp.sum(swap(partial, "zh").astype(F32), axis=0)
    square_sum = total[2 * own_units] + total[2 * own_units + 2]
    score = total[2 * own_units + 1] + total[2 * own_units + 3]
    scale = lax.rsqrt(square_sum / D + 1e-05)
    weight = jax.nn.sigmoid(score * scale)
    gate = total[:own_units] * scale[None, :]
    up = total[own_units : 2 * own_units] * scale[None, :]
    hidden = (jax.nn.silu(gate) * up).astype(BF)
    hidden = lax.all_gather(hidden, "zh", axis=0, tiled=True)

    terms = lax.dot_general(
        hidden, down_r, (((0,), (1,)), ((), ())), preferred_element_type=F32
    ).astype(BF)
    terms = swap(terms.transpose(1, 0, 2), NEAR)
    expert_out = jnp.sum(terms.astype(F32), axis=0)
    expert_out = (expert_out * weight[:, None]).astype(BF)
    returned = swap(expert_out.reshape(experts, capacity, width), BRANCH).reshape(rows, width)
    mixed = lax.dot_general(table, returned, (((0,), (0,)), ((), ())), preferred_element_type=F32)
    return (attended_f.astype(BF), mixed.astype(BF))


def solution(mesh):
    fine = Mesh(mesh.devices.reshape(4, 4, 4, 4, 2), ("zl", "y", "zh", "x", "c"))
    shard = ("zh", "x", "c")
    in_specs = (
        P(BRANCH, shard),
        P(BRANCH, shard),
        P(BRANCH, None, shard),
        P(shard),
        P(shard, None),
        P(BRANCH, None),
        P(BRANCH, shard, None),
        P(BRANCH, shard, None),
        P(BRANCH, None, shard),
    )
    out_specs = (P(BRANCH, shard), P(BRANCH, shard))
    return jax.shard_map(body, mesh=fine, in_specs=in_specs, out_specs=out_specs, check_vma=False)
```

time: 805 us -> 284 us (0.35)
  waiting for transfers between devices: 407 us -> 66.6 us
  blocking collectives: 325 us -> 137 us
  starting transfers between devices: 26.5 us -> 43.6 us
    psum x2 -> x0, blocking collectives: 181 us -> none  [the longest x1 94.5 us: body(): square_sum = lax.psum(squares, 'shard')]
    unnamed x4 -> x1, waiting for transfers between devices: 140 us -> 0.02 us
    psum x1 -> x0, waiting for transfers between devices: 103 us -> none  [body(): lax.psum(attn_weights[0].astype(jnp.float32).astype(jnp.bfloat16), 'branch')]
    all_gather x1, waiting for transfers between devices: 85.5 us -> 0.01 us  [body(): near = lax.all_gather(received, NEAR, axis=0, tiled=False)]
    all_gather x1 -> x2, blocking collectives: 62.1 us -> 42.6 us  [the longest x1 25.9 us: body(): hidden = lax.all_gather(hidden, 'zh', axis=0, tiled=True)]
    all_to_all x4 -> x7, starting transfers between devices: 26.4 us -> 43.5 us  [swap(): lax.all_to_all(values, axes, split_axis=0, concat_axis=0, tiled=False)]
    all_to_all x1 -> x3, blocking collectives: 81.9 us -> 94.8 us  [swap(): lax.all_to_all(values, axes, split_axis=0, concat_axis=0, tiled=False)]
    all_to_all x4 -> x7, waiting for transfers between devices: 78.7 us -> 66.6 us  [swap(): lax.all_to_all(values, axes, split_axis=0, concat_axis=0, tiled=False)]
  transfers between devices with their start and end apart: 7 -> 8, of which waited for: 5 -> 5; matrix products, arithmetic and copies ran while one was open for 2% -> 4% of each run, Pallas kernels for 0% -> 0%
where the time goes in v1:
time: 284 us; the launch traced here: 283 us
  blocking collectives  137 us (48%)
  waiting for transfers between devices  66.6 us (23%)
  starting transfers between devices  43.6 us (15%)
  between operations  14.3 us (5%)
  local copies, waits for them, and re-layouts  9.49 us (3%)
  matrix products  7.77 us (3%)
  other arithmetic  3.57 us (1%)
    all_to_all x3, blocking collectives, swap(): lax.all_to_all(values, axes, split_axis=0, concat_axis=0, tiled=False)  94.8 us
    all_to_all x7, waiting for transfers between devices, swap(): lax.all_to_all(values, axes, split_axis=0, concat_axis=0, tiled=False)  66.6 us
    all_to_all x7, starting transfers between devices, swap(): lax.all_to_all(values, axes, split_axis=0, concat_axis=0, tiled=False)  43.5 us
    all_gather x1, blocking collectives, body(): hidden = lax.all_gather(hidden, 'zh', axis=0, tiled=True)  25.9 us
    all_gather x1, blocking collectives, body(): lax.all_gather(ctx, NEAR, axis=1, tiled=False).reshape(heads, token_count)  16.7 us
  transfers between devices with their start and end apart: 8, of which 5 were waited for; matrix products, arithmetic and copies ran while one was open for 4% of the time, Pallas kernels for 0%

profile of v1, /device:TPU:1, one launch (start us, length us, event | category | flops | bytes accessed | tf_op | source)
XLA Modules:
  0.0 282.8 jit_solution(9065529929451833855)
XLA Ops:
  7.2 22.8 %all_to_all.50 = bf16[16,128,128]{2,1,0:T(8,128)(2,1)S(1)} all-to-all(bf16[16,128,128]{2,1,0:T(8,128)(2,1)} %bitcast.98), channel_id=1, replica_groups=mesh['zl'=4,'y'=4,'zh'=4,'x'=4,'c'=2] {'zl','y'}, dimensions={0} | all-to-all | bytes 1048576 | tf_op jit(solution)/shard_map/all_to_all | solution.py:15
  30.0 1.4 broadcast_in_dim.11
  31.4 12.2 %all-to-all-start.2 = ((bf16[4,64,128]{2,1,0:T(8,128)(2,1)}), bf16[4,64,128]{2,1,0:T(8,128)(2,1)S(1)}, u32[]{:S(2)}, u32[]{:S(2)}) async-start(bf16[4,64,128]{2,1,0:T(8,128)(2,1)} %broadcast_in_dim.11), calls=%async_computation.2 | async-start | bytes 131072 | tf_op jit(solution)/shard_map/all_to_all | solution.py:15
  43.7 11.7 %all-to-all-done.2 = bf16[4,64,128]{2,1,0:T(8,128)(2,1)S(1)} async-done(((bf16[4,64,128]{2,1,0:T(8,128)(2,1)}), bf16[4,64,128]{2,1,0:T(8,128)(2,1)S(1)}, u32[]{:S(2)}, u32[]{:S(2)}) %all-to-all-start.2) | async-done | bytes 65568 | tf_op jit(solution)/shard_map/all_to_all | solution.py:15
  56.3 5.1 %all-to-all-start.1 = ((bf16[16,128,128]{2,1,0:T(8,128)(2,1)}), bf16[16,128,128]{2,1,0:T(8,128)(2,1)S(1)}, u32[]{:S(2)}, u32[]{:S(2)}) async-start(bf16[16,128,128]{2,1,0:T(8,128)(2,1)} %broadcast_in_dim.10), calls=%async_computation.1 | async-start | bytes 1048576 | tf_op jit(solution)/shard_map/all_to_all | solution.py:15
  63.3 16.7 %all-gather = bf16[4,512,128]{2,1,0:T(8,128)(2,1)S(1)} all-gather(bf16[4,64,128]{2,1,0:T(8,128)(2,1)S(1)} %all-to-all-done.2), channel_id=2, replica_groups=mesh['zl'=4,'y'=4,'zh'=4,'x'=4,'c'=2] {'x','c'}, dimensions={1}, use_global_device_ids=true | all-gather | bytes 589824 | tf_op jit(solution)/shard_map/all_gather | solution.py:53
  81.5 15.1 %all_to_all.51 = bf16[16,32,128]{2,1,0:T(8,128)(2,1)} all-to-all(bf16[16,32,128]{2,1,0:T(8,128)(2,1)S(1)} %fusion.10), channel_id=1, replica_groups=mesh['zl'=4,'y'=4,'zh'=4,'x'=4,'c'=2] {'zl','y'}, dimensions={0} | all-to-all | bytes 262144 | tf_op jit(solution)/shard_map/all_to_all | solution.py:15
  96.6 1.6 copy.57
  98.2 5.4 %all-to-all-start.4 = ((bf16[8,704,128]{2,1,0:T(8,128)(2,1)}), bf16[8,704,128]{2,1,0:T(8,128)(2,1)S(1)}, u32[]{:S(2)}, u32[]{:S(2)}) async-start(bf16[8,704,128]{2,1,0:T(8,128)(2,1)} %bitcast.18), calls=%async_computation.4 | async-start | bytes 2883584 | tf_op jit(solution)/shard_map/all_to_all | solution.py:15
  103.5 1.5 copy.58
  105.1 22.1 %all-to-all-done.4 = bf16[8,704,128]{2,1,0:T(8,128)(2,1)S(1)} async-done(((bf16[8,704,128]{2,1,0:T(8,128)(2,1)}), bf16[8,704,128]{2,1,0:T(8,128)(2,1)S(1)}, u32[]{:S(2)}, u32[]{:S(2)}) %all-to-all-start.4) | async-done | bytes 1441824 | tf_op jit(solution)/shard_map/all_to_all | solution.py:15
  127.2 4.2 %all-to-all-start.5 = ((bf16[8,704,128]{2,1,0:T(8,128)(2,1)}), bf16[8,704,128]{2,1,0:T(8,128)(2,1)S(1)}, u32[]{:S(2)}, u32[]{:S(2)}) async-start(bf16[8,704,128]{2,1,0:T(8,128)(2,1)} %bitcast.24), calls=%async_computation.5 | async-start | bytes 2883584 | tf_op jit(solution)/shard_map/all_to_all | solution.py:15
  131.5 2.1 slice.72
  135.0 2.1 fusion
  137.1 13.7 %all-to-all-done.5 = bf16[8,704,128]{2,1,0:T(8,128)(2,1)S(1)} async-done(((bf16[8,704,128]{2,1,0:T(8,128)(2,1)}), bf16[8,704,128]{2,1,0:T(8,128)(2,1)S(1)}, u32[]{:S(2)}, u32[]{:S(2)}) %all-to-all-start.5) | async-done | bytes 1441824 | tf_op jit(solution)/shard_map/all_to_all | solution.py:15
  150.7 2.1 fusion.1
  153.0 56.9 %all_to_all.52 = bf16[4,368,384]{2,1,0:T(8,128)(2,1)S(1)} all-to-all(bf16[4,368,384]{2,1,0:T(8,128)(2,1)S(1)} %pad_maximum_fusion), channel_id=1, replica_groups=mesh['zl'=4,'y'=4,'zh'=4,'x'=4,'c'=2] {'zh'}, dimensions={0} | all-to-all | bytes 2260992 | tf_op jit(solution)/shard_map/all_to_all | solution.py:15
  209.8 7.1 %all-to-all-start.7 = ((bf16[8,704,128]{2,1,0:T(8,128)(2,1)}), bf16[8,704,128]{2,1,0:T(8,128)(2,1)S(1)}, u32[]{:S(2)}, u32[]{:S(2)}) async-start(bf16[8,704,128]{2,1,0:T(8,128)(2,1)} %bitcast.30), calls=%async_computation.7 | async-start | bytes 2883584 | tf_op jit(solution)/shard_map/all_to_all | solution.py:15
  217.2 25.9 %all_gather.19 = bf16[704,384]{1,0:T(8,128)(2,1)S(1)} all-gather(bf16[176,384]{1,0:T(8,128)(2,1)S(1)} %fusion.7), channel_id=1, replica_groups=mesh['zl'=4,'y'=4,'zh'=4,'x'=4,'c'=2] {'zh'}, dimensions={0}, use_global_device_ids=true | all-gather | bytes 675840 | tf_op jit(solution)/shard_map/all_gather | solution.py:100
  243.1 1.7 fusion.2
  244.8 4.8 %all-to-all-start.8 = ((bf16[8,384,128]{2,1,0:T(8,128)(2,1)}), bf16[8,384,128]{2,1,0:T(8,128)(2,1)S(1)}, u32[]{:S(2)}, u32[]{:S(2)}) async-start(bf16[8,384,128]{2,1,0:T(8,128)(2,1)} %fusion.2), calls=%async_computation.8 | async-start | bytes 1572864 | tf_op jit(solution)/shard_map/all_to_all | solution.py:15
  249.7 12.2 %all-to-all-done.8 = bf16[8,384,128]{2,1,0:T(8,128)(2,1)S(1)} async-done(((bf16[8,384,128]{2,1,0:T(8,128)(2,1)}), bf16[8,384,128]{2,1,0:T(8,128)(2,1)S(1)}, u32[]{:S(2)}, u32[]{:S(2)}) %all-to-all-start.8) | async-done | bytes 786464 | tf_op jit(solution)/shard_map/all_to_all | solution.py:15
  262.8 4.7 %all-to-all-start.9 = ((bf16[16,24,128]{2,1,0:T(8,128)(2,1)}), bf16[16,24,128]{2,1,0:T(8,128)(2,1)S(1)}, u32[]{:S(2)}, u32[]{:S(2)}) async-start(bf16[16,24,128]{2,1,0:T(8,128)(2,1)} %multiply_convert_fusion), calls=%async_computation.9 | async-start | bytes 196608 | tf_op jit(solution)/shard_map/all_to_all | solution.py:15
  268.2 6.9 %all-to-all-done.9 = bf16[16,24,128]{2,1,0:T(8,128)(2,1)S(1)} async-done(((bf16[16,24,128]{2,1,0:T(8,128)(2,1)}), bf16[16,24,128]{2,1,0:T(8,128)(2,1)S(1)}, u32[]{:S(2)}, u32[]{:S(2)}) %all-to-all-start.9) | async-done | bytes 98336 | tf_op jit(solution)/shard_map/all_to_all | solution.py:15
  (67 shorter events, 8.5 us)
Async XLA Ops:
  7.2 73.2 %copy-start = (bf16[128,16]{0,1:T(8,128)(2,1)S(1)}, bf16[128,16]{0,1:T(8,128)(2,1)}, u32[]{:S(2)}) copy-start(bf16[128,16]{0,1:T(8,128)(2,1)} %param.13) | copy-start | bytes 12292
  30.0 31.5 %copy-start.4 = (s32[128,2]{0,1:T(2,128)S(1)}, s32[128,2]{0,1:T(2,128)}, u32[]{:S(2)}) copy-start(s32[128,2]{0,1:T(2,128)} %param.14) | copy-start | bytes 3076
  30.0 31.9 %copy-start.3 = (bf16[128,128]{1,0:T(8,128)(2,1)S(1)}, bf16[128,128]{1,0:T(8,128)(2,1)}, u32[]{:S(2)}) copy-start(bf16[128,128]{1,0:T(8,128)(2,1)} %param.9) | copy-start | bytes 98308
  30.0 32.0 %copy-start.5 = (bf16[128]{0:T(256)(128)(2,1)S(1)}, bf16[128]{0:T(256)(128)(2,1)}, u32[]{:S(2)}) copy-start(bf16[128]{0:T(256)(128)(2,1)} %param.12) | copy-start | bytes 772
  31.4 24.0 %all-to-all-start.2 = ((bf16[4,64,128]{2,1,0:T(8,128)(2,1)}), bf16[4,64,128]{2,1,0:T(8,128)(2,1)S(1)}, u32[]{:S(2)}, u32[]{:S(2)}) async-start(bf16[4,64,128]{2,1,0:T(8,128)(2,1)} %broadcast_in_dim.11), calls=%async_computation.2 | async-start | bytes 131072 | tf_op jit(solution)/shard_map/all_to_all | solution.py:15
  56.3 23.7 %all-to-all-start.1 = ((bf16[16,128,128]{2,1,0:T(8,128)(2,1)}), bf16[16,128,128]{2,1,0:T(8,128)(2,1)S(1)}, u32[]{:S(2)}, u32[]{:S(2)}) async-start(bf16[16,128,128]{2,1,0:T(8,128)(2,1)} %broadcast_in_dim.10), calls=%async_computation.1 | async-start | bytes 1048576 | tf_op jit(solution)/shard_map/all_to_all | solution.py:15
  61.5 70.0 %all-gather.4.cloned.1.call-start = ((), (), s32[]{:S(2)}) async-start(), calls=%async_computation.10 | async-start | bytes 1179648 | tf_op jit(solution)/shard_map/all_gather | solution.py:74
  80.0 16.6 %copy-start.1 = (bf16[1,128,5632]{2,1,0:T(8,128)(2,1)S(1)}, bf16[1,128,5632]{2,1,0:T(8,128)(2,1)}, u32[]{:S(2)}) copy-start(bf16[1,128,5632]{2,1,0:T(8,128)(2,1)} %param.15) | copy-start | bytes 4325380
  98.1 5.4 %copy-start.2 = (bf16[1,128,5632]{2,1,0:T(8,128)(2,1)S(1)}, bf16[1,128,5632]{2,1,0:T(8,128)(2,1)}, u32[]{:S(2)}) copy-start(bf16[1,128,5632]{2,1,0:T(8,128)(2,1)} %param.16) | copy-start | bytes 4325380
  98.2 29.0 %all-to-all-start.4 = ((bf16[8,704,128]{2,1,0:T(8,128)(2,1)}), bf16[8,704,128]{2,1,0:T(8,128)(2,1)S(1)}, u32[]{:S(2)}, u32[]{:S(2)}) async-start(bf16[8,704,128]{2,1,0:T(8,128)(2,1)} %bitcast.18), calls=%async_computation.4 | async-start | bytes 2883584 | tf_op jit(solution)/shard_map/all_to_all | solution.py:15
  127.2 23.5 %all-to-all-start.5 = ((bf16[8,704,128]{2,1,0:T(8,128)(2,1)}), bf16[8,704,128]{2,1,0:T(8,128)(2,1)S(1)}, u32[]{:S(2)}, u32[]{:S(2)}) async-start(bf16[8,704,128]{2,1,0:T(8,128)(2,1)} %bitcast.24), calls=%async_computation.5 | async-start | bytes 2883584 | tf_op jit(solution)/shard_map/all_to_all | solution.py:15
  209.8 33.3 %all-to-all-start.7 = ((bf16[8,704,128]{2,1,0:T(8,128)(2,1)}), bf16[8,704,128]{2,1,0:T(8,128)(2,1)S(1)}, u32[]{:S(2)}, u32[]{:S(2)}) async-start(bf16[8,704,128]{2,1,0:T(8,128)(2,1)} %bitcast.30), calls=%async_computation.7 | async-start | bytes 2883584 | tf_op jit(solution)/shard_map/all_to_all | solution.py:15
  244.8 17.1 %all-to-all-start.8 = ((bf16[8,384,128]{2,1,0:T(8,128)(2,1)}), bf16[8,384,128]{2,1,0:T(8,128)(2,1)S(1)}, u32[]{:S(2)}, u32[]{:S(2)}) async-start(bf16[8,384,128]{2,1,0:T(8,128)(2,1)} %fusion.2), calls=%async_computation.8 | async-start | bytes 1572864 | tf_op jit(solution)/shard_map/all_to_all | solution.py:15
  262.8 12.3 %all-to-all-start.9 = ((bf16[16,24,128]{2,1,0:T(8,128)(2,1)}), bf16[16,24,128]{2,1,0:T(8,128)(2,1)S(1)}, u32[]{:S(2)}, u32[]{:S(2)}) async-start(bf16[16,24,128]{2,1,0:T(8,128)(2,1)} %multiply_convert_fusion), calls=%async_computation.9 | async-start | bytes 196608 | tf_op jit(solution)/shard_map/all_to_all | solution.py:15
Sparse Core Ops, SparseCore 0:
  96.7 23.9 all-gather.3

commit v2 on v1

--- a/solution.py
+++ b/solution.py
@@ -17,6 +17,83 @@
 
 def spread(values, axes, count):
     return swap(jnp.broadcast_to(values[None], (count,) + values.shape), axes)
+
+
+def at(values, index):
+    return lax.dynamic_index_in_dim(values, index, 0, keepdims=False)
+
+
+def shift(values, axis, step, count):
+    return lax.ppermute(values, axis, [(i, (i + step) % count) for i in range(count)])
+
+
+def add(*terms):
+    total = terms[0].astype(F32)
+    for term in terms[1:]:
+        total = total + term.astype(F32)
+    return total
+
+
+def pair_up(blocks):
+    core = lax.axis_index("c")
+    kept = lax.dynamic_index_in_dim(blocks, core, 1, keepdims=False)
+    other = lax.dynamic_index_in_dim(blocks, 1 - core, 1, keepdims=False)
+    return jnp.stack([kept, shift(other, "c", 1, 2)], axis=1)
+
+
+def relay_x(both):
+    x = lax.axis_index("x")
+    return [at(both, x)] + [shift(at(both, (x + k) % 4), "x", k, 4) for k in (1, 2, 3)]
+
+
+def in_order(relaid):
+    x, core = lax.axis_index("x"), lax.axis_index("c")
+    held = jnp.zeros((8,) + relaid[0].shape[1:], relaid[0].dtype)
+    for k in range(4):
+        for j in range(2):
+            sender = 2 * ((x + 4 - k) % 4) + (core + j) % 2
+            held = lax.dynamic_update_index_in_dim(held, relaid[k][j], sender, 0)
+    return held
+
+
+def add(*terms):
+    total = terms[0].astype(F32)
+    for term in terms[1:]:
+        total = total + term.astype(F32)
+    return total
+
+
+def pair_up(blocks):
+    core = lax.axis_index("c")
+    kept = lax.dynamic_index_in_dim(blocks, core, 1, keepdims=False)
+    other = lax.dynamic_index_in_dim(blocks, 1 - core, 1, keepdims=False)
+    return jnp.stack([kept, shift(other, "c", 1, 2)], axis=1)
+
+
+def relay_x(both):
+    x = lax.axis_index("x")
+    return [at(both, x)] + [shift(at(both, (x + k) % 4), "x", k, 4) for k in (1, 2, 3)]
+
+
+def gather_far(values):
+    z = lax.axis_index("zh")
+    held = jnp.zeros((4,) + values.shape, values.dtype)
+    for k in range(4):
+        came = shift(values, "zh", k, 4) if k else values
+        held = lax.dynamic_update_index_in_dim(held, came, (z + 4 - k) % 4, 0)
+    return held
+
+
+def sum_far(gate, up):
+    z = lax.axis_index("zh")
+    g = [at(gate, (z + k) % 4) for k in range(4)]
+    u = [at(up, (z + k) % 4) for k in range(4)]
+    n, m = g[0].shape[0], u[0].shape[0]
+    ahead = shift(jnp.concatenate([g[2], u[1]]), "zh", 1, 4)
+    back = shift(jnp.concatenate([u[2], g[3]]), "zh", 3, 4)
+    ahead_two = shift(add(g[1], ahead[:n]).astype(BF), "zh", 1, 4)
+    back_two = shift(add(u[3], back[:m]).astype(BF), "zh", 3, 4)
+    return add(g[0], back[m:], ahead_two), add(u[0], ahead[n:], back_two)
 
 
 def halves(values):
@@ -41,15 +118,23 @@
     near_units = hidden_units // 8
     own_units = near_units // 4
 
-    gate_r = swap(gate_w[0].T.reshape(8, near_units, width), NEAR)
-    up_r = swap(up_w[0].T.reshape(8, near_units, width), NEAR)
-    down_r = swap(down_w[0].reshape(8, near_units, width), NEAR)
+    blocks = jnp.concatenate(
+        [
+            gate_w[0].T.reshape(4, 2, near_units, width),
+            up_w[0].T.reshape(4, 2, near_units, width),
+        ],
+        axis=2,
+    )
+    both = pair_up(blocks)
 
     parts = swap(attn_weights[0].reshape(experts, heads // experts, width), BRANCH)
     chunk = (jnp.sum(parts.astype(F32), axis=0) / experts).astype(BF)
+    relaid = relay_x(both)
+    ctx = lax.all_gather(context.T, "zh", axis=0, tiled=False)
+    chunk, ctx, relaid[1], relaid[3] = lax.optimization_barrier((chunk, ctx, relaid[1], relaid[3]))
     merged = spread(chunk, BRANCH, experts).reshape(heads, width)
-
-    ctx = spread(context.T, "zh", 4)
+    merged, relaid[2] = lax.optimization_barrier((merged, relaid[2]))
+
     ctx = lax.all_gather(ctx, NEAR, axis=1, tiled=False).reshape(heads, token_count)
     attention_out = lax.dot_general(ctx, merged, (((0,), (0,)), ((), ())), preferred_element_type=F32)
     attended_f = tokens.astype(F32) + attention_out
@@ -68,34 +153,32 @@
     own = jnp.eye(experts, dtype=F32)[:, None, None, :]
     score_part = jnp.sum(extra[..., 1:] * own, axis=3)
     extra = jnp.concatenate([extra[..., 0], score_part], axis=2).transpose(0, 2, 1).astype(BF)
-    extra = jnp.pad(extra, ((0, 0), (0, 4), (0, width - capacity)))
+    extra = jnp.pad(extra.reshape(experts, 1, 4 * capacity), ((0, 0), (0, 0), (0, width - 4 * capacity)))
     sent = jnp.concatenate([sent.reshape(experts, capacity, width), extra], axis=1)
     received = swap(sent, BRANCH)
+    received = jnp.concatenate([received[:, :capacity].reshape(rows, width), received[:, capacity]])
+    received, weights = lax.optimization_barrier((received, in_order(relaid)))
     near = lax.all_gather(received, NEAR, axis=0, tiled=False)
-    piece = near[:, :, :capacity].reshape(8, rows, width)
-    extra = jnp.sum(near[:, :, capacity : capacity + 4, :capacity].astype(F32), axis=0)
-    extra = extra.transpose(1, 0, 2).reshape(4, rows)
+    extra = jnp.sum(near[:, rows:, : 4 * capacity].astype(F32), axis=0)
+    extra = extra.reshape(experts, 4, capacity).transpose(1, 0, 2).reshape(4, rows)
     extra_high, extra_low = halves(jnp.stack([extra[0] + extra[1], extra[2] + extra[3]]))
     extra = jnp.concatenate([extra_high, extra_low, jnp.zeros((12, rows), BF)])
 
-    product = (((0, 2), (0, 2)), ((), ()))
-    gate = lax.dot_general(gate_r, piece, product, preferred_element_type=F32).astype(BF)
-    up = lax.dot_general(up_r, piece, product, preferred_element_type=F32).astype(BF)
-    partial = jnp.concatenate(
-        [
-            gate.reshape(4, own_units, rows),
-            up.reshape(4, own_units, rows),
-            jnp.broadcast_to(extra[None], (4, 16, rows)),
-        ],
-        axis=1,
+    down_blocks, near = lax.optimization_barrier((down_w[0], near))
+    down_r = swap(down_blocks.reshape(8, near_units, width), NEAR)
+
+    product = lax.dot_general(
+        weights, near, (((0, 2), (0, 2)), ((), ())), preferred_element_type=F32
     )
-    total = jnp.sum(swap(partial, "zh").astype(F32), axis=0)
-    square_sum = total[2 * own_units] + total[2 * own_units + 2]
-    score = total[2 * own_units + 1] + total[2 * own_units + 3]
+    product = product[:, :rows].astype(BF).reshape(2, 4, own_units, rows)
+    extra = jnp.broadcast_to(extra[None], (4, 16, rows))
+    gate, up = sum_far(product[0], jnp.concatenate([product[1], extra], axis=1))
+    square_sum = up[own_units] + up[own_units + 2]
+    score = up[own_units + 1] + up[own_units + 3]
     scale = lax.rsqrt(square_sum / D + 1e-05)
     weight = jax.nn.sigmoid(score * scale)
-    gate = total[:own_units] * scale[None, :]
-    up = total[own_units : 2 * own_units] * scale[None, :]
+    gate = gate * scale[None, :]
+    up = up[:own_units] * scale[None, :]
     hidden = (jax.nn.silu(gate) * up).astype(BF)
     hidden = lax.all_gather(hidden, "zh", axis=0, tiled=True)
 

time: 284 us -> 229 us (0.81)
  blocking collectives: 137 us -> 76.2 us
  starting transfers between devices: 43.6 us -> 69 us
  waiting for transfers between devices: 66.6 us -> 50 us
  between operations: 14.3 us -> 1.38 us
  other arithmetic: 3.57 us -> 10.3 us
  local copies, waits for them, and re-layouts: 9.49 us -> 13.9 us
    all_to_all x3 -> x0, blocking collectives: 94.8 us -> none  [swap(): lax.all_to_all(values, axes, split_axis=0, concat_axis=0, tiled=False)]
    all_to_all x7 -> x6, waiting for transfers between devices: 66.6 us -> 22.9 us  [swap(): lax.all_to_all(values, axes, split_axis=0, concat_axis=0, tiled=False)]
    ppermute x0 -> x8, starting transfers between devices: none -> 37.2 us  [shift(): lax.ppermute(values, axis, [(i, (i + step) % count) for i in range(count)])]
    all_gather x0 -> x2, blocking collectives: none -> 34.6 us  [the longest x1 19.6 us: body(): ctx = lax.all_gather(context.T, 'zh', axis=0, tiled=False)]
    ppermute x0 -> x8, waiting for transfers between devices: none -> 27.1 us  [shift(): lax.ppermute(values, axis, [(i, (i + step) % count) for i in range(count)])]
    all_to_all x7 -> x6, starting transfers between devices: 43.5 us -> 31.8 us  [swap(): lax.all_to_all(values, axes, split_axis=0, concat_axis=0, tiled=False)]
    unnamed x15 -> x28, local copies, waits for them, and re-layouts: 0.97 us -> 6.1 us
    dynamic_update_slice x0 -> x8, local copies, waits for them, and re-layouts: none -> 4.35 us  [in_order(): held = lax.dynamic_update_index_in_dim(held, relaid[k][j], sender, 0)]
  transfers between devices with their start and end apart: 8 -> 14, of which waited for: 5 -> 6; matrix products, arithmetic and copies ran while one was open for 4% -> 6% of each run, Pallas kernels for 0% -> 0%
where the time goes in v2:
time: 229 us; the launch traced here: 228 us
  blocking collectives  76.2 us (33%)
  starting transfers between devices  69 us (30%)
  waiting for transfers between devices  50 us (22%)
  local copies, waits for them, and re-layouts  13.9 us (6%)
  other arithmetic  10.3 us (4%)
  matrix products  6.78 us (3%)
    ppermute x8, starting transfers between devices, shift(): lax.ppermute(values, axis, [(i, (i + step) % count) for i in range(count)])  37.2 us
    all_to_all x6, starting transfers between devices, swap(): lax.all_to_all(values, axes, split_axis=0, concat_axis=0, tiled=False)  31.8 us
    ppermute x8, waiting for transfers between devices, shift(): lax.ppermute(values, axis, [(i, (i + step) % count) for i in range(count)])  27.1 us
    all_gather x1, blocking collectives, body(): hidden = lax.all_gather(hidden, 'zh', axis=0, tiled=True)  23 us
    all_to_all x6, waiting for transfers between devices, swap(): lax.all_to_all(values, axes, split_axis=0, concat_axis=0, tiled=False)  22.9 us
    all_gather x1, blocking collectives, body(): ctx = lax.all_gather(context.T, 'zh', axis=0, tiled=False)  19.6 us
    all_gather x1, blocking collectives, body(): lax.all_gather(ctx, NEAR, axis=1, tiled=False).reshape(heads, token_count)  18.6 us
    all_gather x1, blocking collectives, body(): near = lax.all_gather(received, NEAR, axis=0, tiled=False)  15 us
  transfers between devices with their start and end apart: 14, of which 6 were waited for; matrix products, arithmetic and copies ran while one was open for 6% of the time, Pallas kernels for 0%

profile of v2, /device:TPU:1, one launch (start us, length us, event | category | flops | bytes accessed | tf_op | source)
XLA Modules:
  0.0 227.5 jit_solution(658180626381771560)
XLA Ops:
  6.1 8.9 %collective-permute-start = (bf16[4,1408,128]{2,1,0:T(8,128)(2,1)}, bf16[4,1408,128]{2,1,0:T(8,128)(2,1)S(1)}, u32[]{:S(2)}, u32[]{:S(2)}) collective-permute-start(bf16[4,1408,128]{2,1,0:T(8,128)(2,1)} %get-tuple-element.42), channel_id=1, source_target_pairs={{0,1},{1,0},{2,3},{3,2},{4,5},{5,4},{6,7},{7,6},{8,9},{9,8},{10,11... | collective-permute-start | bytes 4325384 | tf_op jit(solution)/shard_map/ppermute | solution.py:27
  15.1 3.6 %all-to-all-start = ((bf16[16,128,128]{2,1,0:T(8,128)(2,1)}), bf16[16,128,128]{2,1,0:T(8,128)(2,1)S(1)}, u32[]{:S(2)}, u32[]{:S(2)}) async-start(bf16[16,128,128]{2,1,0:T(8,128)(2,1)} %bitcast.135), calls=%async_computation | async-start | bytes 1048576 | tf_op jit(solution)/shard_map/all_to_all | solution.py:15
  22.9 2.5 %collective-permute-start.1 = (bf16[2,1408,128]{2,1,0:T(8,128)(2,1)}, bf16[2,1408,128]{2,1,0:T(8,128)(2,1)S(1)}, u32[]{:S(2)}, u32[]{:S(2)}) collective-permute-start(bf16[2,1408,128]{2,1,0:T(8,128)(2,1)} %get-tuple-element.39), channel_id=1, source_target_pairs={{0,2},{2,4},{4,6},{6,0},{1,3},{3,5},{5,7},{7,1},{8,10},{10,12},{12... | collective-permute-start | bytes 2162696 | tf_op jit(solution)/shard_map/ppermute | solution.py:27
  25.4 4.0 %collective-permute-start.2 = (bf16[2,1408,128]{2,1,0:T(8,128)(2,1)}, bf16[2,1408,128]{2,1,0:T(8,128)(2,1)S(1)}, u32[]{:S(2)}, u32[]{:S(2)}) collective-permute-start(bf16[2,1408,128]{2,1,0:T(8,128)(2,1)} %get-tuple-element.40), channel_id=1, source_target_pairs={{0,6},{2,0},{4,2},{6,4},{1,7},{3,1},{5,3},{7,5},{8,14},{10,8},{12,... | collective-permute-start | bytes 2162696 | tf_op jit(solution)/shard_map/ppermute | solution.py:27
  29.4 19.6 %all-gather = bf16[256,128]{1,0:T(8,128)(2,1)S(1)} all-gather(bf16[64,128]{1,0:T(8,128)(2,1)S(1)} %bitcast.143), channel_id=2, replica_groups=mesh['zl'=4,'y'=4,'zh'=4,'x'=4,'c'=2] {'zh'}, dimensions={0}, use_global_device_ids=true | all-gather | bytes 81920 | tf_op jit(solution)/shard_map/all_gather | solution.py:133
  49.1 3.4 %collective-permute-start.3 = (bf16[2,1408,128]{2,1,0:T(8,128)(2,1)}, bf16[2,1408,128]{2,1,0:T(8,128)(2,1)}, u32[]{:S(2)}, u32[]{:S(2)}) collective-permute-start(bf16[2,1408,128]{2,1,0:T(8,128)(2,1)} %get-tuple-element.41), channel_id=1, source_target_pairs={{0,4},{2,6},{4,0},{6,2},{1,5},{3,7},{5,1},{7,3},{8,12},{10,14},{12... | collective-permute-start | bytes 2162696 | tf_op jit(solution)/shard_map/ppermute | solution.py:27
  53.7 7.1 %all-to-all-start.1 = ((bf16[16,128,128]{2,1,0:T(8,128)(2,1)}), bf16[16,128,128]{2,1,0:T(8,128)(2,1)S(1)}, u32[]{:S(2)}, u32[]{:S(2)}) async-start(bf16[16,128,128]{2,1,0:T(8,128)(2,1)} %broadcast_in_dim.19), calls=%async_computation.1 | async-start | bytes 1048576 | tf_op jit(solution)/shard_map/all_to_all | solution.py:15
  62.1 18.6 %all-gather.1 = bf16[4,512,128]{2,1,0:T(8,128)(2,1)} all-gather(bf16[4,64,128]{2,1,0:T(8,128)(2,1)S(1)} %bitcast.139), channel_id=3, replica_groups=mesh['zl'=4,'y'=4,'zh'=4,'x'=4,'c'=2] {'x','c'}, dimensions={1}, use_global_device_ids=true | all-gather | bytes 589824 | tf_op jit(solution)/shard_map/all_gather | solution.py:138
  84.7 7.2 %all-to-all-start.2 = ((bf16[16,25,128]{2,1,0:T(8,128)(2,1)}), bf16[16,25,128]{2,1,0:T(8,128)(2,1)S(1)}, u32[]{:S(2)}, u32[]{:S(2)}) async-start(bf16[16,25,128]{2,1,0:T(8,128)(2,1)} %fusion.33), calls=%async_computation.2 | async-start | bytes 262144 | tf_op jit(solution)/shard_map/all_to_all | solution.py:15
  96.1 3.8 %all-to-all-done.2 = bf16[16,25,128]{2,1,0:T(8,128)(2,1)S(1)} async-done(((bf16[16,25,128]{2,1,0:T(8,128)(2,1)}), bf16[16,25,128]{2,1,0:T(8,128)(2,1)S(1)}, u32[]{:S(2)}, u32[]{:S(2)}) %all-to-all-start.2) | async-done | bytes 102432 | tf_op jit(solution)/shard_map/all_to_all | solution.py:15
  99.9 15.0 %all-gather.2 = bf16[3200,128]{1,0:T(8,128)(2,1)S(1)} all-gather(bf16[400,128]{1,0:T(8,128)(2,1)S(1)} %pad_maximum_fusion.2), channel_id=4, replica_groups=mesh['zl'=4,'y'=4,'zh'=4,'x'=4,'c'=2] {'x','c'}, dimensions={0}, use_global_device_ids=true | all-gather | bytes 921600 | tf_op jit(solution)/shard_map/all_gather | solution.py:161
  117.8 4.0 %collective-permute-start.4 = (bf16[368,384]{1,0:T(8,128)(2,1)S(1)}, bf16[368,384]{1,0:T(8,128)(2,1)}, u32[]{:S(2)}, u32[]{:S(2)}) collective-permute-start(bf16[368,384]{1,0:T(8,128)(2,1)S(1)} %pad_maximum_fusion), channel_id=1, source_target_pairs={{0,24},{8,0},{16,8},{24,16},{1,25},{9,1},{17,9},{25,17},{2,26},{10... | collective-permute-start | bytes 847880 | tf_op jit(solution)/shard_map/ppermute | solution.py:27
  121.9 5.2 %collective-permute-start.5 = (bf16[368,384]{1,0:T(8,128)(2,1)S(1)}, bf16[368,384]{1,0:T(8,128)(2,1)}, u32[]{:S(2)}, u32[]{:S(2)}) collective-permute-start(bf16[368,384]{1,0:T(8,128)(2,1)S(1)} %pad_maximum_fusion.1), channel_id=1, source_target_pairs={{0,8},{8,16},{16,24},{24,0},{1,9},{9,17},{17,25},{25,1},{2,10},{10... | collective-permute-start | bytes 847880 | tf_op jit(solution)/shard_map/ppermute | solution.py:27
  127.1 4.2 %all-to-all-start.3 = ((bf16[8,704,128]{2,1,0:T(8,128)(2,1)}), bf16[8,704,128]{2,1,0:T(8,128)(2,1)S(1)}, u32[]{:S(2)}, u32[]{:S(2)}) async-start(bf16[8,704,128]{2,1,0:T(8,128)(2,1)} %bitcast.43), calls=%async_computation.3 | async-start | bytes 2883584 | tf_op jit(solution)/shard_map/all_to_all | solution.py:15
  131.3 19.1 %collective-permute-done.4 = bf16[368,384]{1,0:T(8,128)(2,1)} collective-permute-done((bf16[368,384]{1,0:T(8,128)(2,1)S(1)}, bf16[368,384]{1,0:T(8,128)(2,1)}, u32[]{:S(2)}, u32[]{:S(2)}) %collective-permute-start.4) | collective-permute-done | bytes 282656 | tf_op jit(solution)/shard_map/ppermute | solution.py:27
  151.4 4.0 %collective-permute-start.7 = (bf16[192,384]{1,0:T(8,128)(2,1)S(1)}, bf16[192,384]{1,0:T(8,128)(2,1)S(1)}, u32[]{:S(2)}, u32[]{:S(2)}) collective-permute-start(bf16[192,384]{1,0:T(8,128)(2,1)S(1)} %fusion.16), channel_id=1, source_target_pairs={{0,24},{8,0},{16,8},{24,16},{1,25},{9,1},{17,9},{25,17},{2,26},{10... | collective-permute-start | bytes 442376 | tf_op jit(solution)/shard_map/ppermute | solution.py:27
  156.3 5.2 %collective-permute-start.6 = (bf16[176,384]{1,0:T(8,128)(2,1)S(1)}, bf16[176,384]{1,0:T(8,128)(2,1)S(1)}, u32[]{:S(2)}, u32[]{:S(2)}) collective-permute-start(bf16[176,384]{1,0:T(8,128)(2,1)S(1)} %fusion.20), channel_id=1, source_target_pairs={{0,8},{8,16},{16,24},{24,0},{1,9},{9,17},{17,25},{25,1},{2,10},{10... | collective-permute-start | bytes 405512 | tf_op jit(solution)/shard_map/ppermute | solution.py:27
  161.5 2.9 %collective-permute-done.7 = bf16[192,384]{1,0:T(8,128)(2,1)S(1)} collective-permute-done((bf16[192,384]{1,0:T(8,128)(2,1)S(1)}, bf16[192,384]{1,0:T(8,128)(2,1)S(1)}, u32[]{:S(2)}, u32[]{:S(2)}) %collective-permute-start.7) | collective-permute-done | bytes 147488 | tf_op jit(solution)/shard_map/ppermute | solution.py:27
  165.5 5.0 %collective-permute-done.6 = bf16[176,384]{1,0:T(8,128)(2,1)S(1)} collective-permute-done((bf16[176,384]{1,0:T(8,128)(2,1)S(1)}, bf16[176,384]{1,0:T(8,128)(2,1)S(1)}, u32[]{:S(2)}, u32[]{:S(2)}) %collective-permute-start.6) | collective-permute-done | bytes 135200 | tf_op jit(solution)/shard_map/ppermute | solution.py:27
  171.5 23.0 %all_gather.27 = bf16[704,384]{1,0:T(8,128)(2,1)S(1)} all-gather(bf16[176,384]{1,0:T(8,128)(2,1)S(1)} %fusion.19), channel_id=1, replica_groups=mesh['zl'=4,'y'=4,'zh'=4,'x'=4,'c'=2] {'zh'}, dimensions={0}, use_global_device_ids=true | all-gather | bytes 675840 | tf_op jit(solution)/shard_map/all_gather | solution.py:183
  196.1 4.7 %all-to-all-start.4 = ((bf16[8,384,128]{2,1,0:T(8,128)(2,1)}), bf16[8,384,128]{2,1,0:T(8,128)(2,1)S(1)}, u32[]{:S(2)}, u32[]{:S(2)}) async-start(bf16[8,384,128]{2,1,0:T(8,128)(2,1)} %fusion.4), calls=%async_computation.4 | async-start | bytes 1572864 | tf_op jit(solution)/shard_map/all_to_all | solution.py:15
  200.9 12.2 %all-to-all-done.4 = bf16[8,384,128]{2,1,0:T(8,128)(2,1)S(1)} async-done(((bf16[8,384,128]{2,1,0:T(8,128)(2,1)}), bf16[8,384,128]{2,1,0:T(8,128)(2,1)S(1)}, u32[]{:S(2)}, u32[]{:S(2)}) %all-to-all-start.4) | async-done | bytes 786464 | tf_op jit(solution)/shard_map/all_to_all | solution.py:15
  214.0 5.0 %all-to-all-start.5 = ((bf16[16,24,128]{2,1,0:T(8,128)(2,1)}), bf16[16,24,128]{2,1,0:T(8,128)(2,1)S(1)}, u32[]{:S(2)}, u32[]{:S(2)}) async-start(bf16[16,24,128]{2,1,0:T(8,128)(2,1)} %multiply_convert_fusion), calls=%async_computation.5 | async-start | bytes 196608 | tf_op jit(solution)/shard_map/all_to_all | solution.py:15
  219.8 6.9 %all-to-all-done.5 = bf16[16,24,128]{2,1,0:T(8,128)(2,1)S(1)} async-done(((bf16[16,24,128]{2,1,0:T(8,128)(2,1)}), bf16[16,24,128]{2,1,0:T(8,128)(2,1)S(1)}, u32[]{:S(2)}, u32[]{:S(2)}) %all-to-all-start.5) | async-done | bytes 98336 | tf_op jit(solution)/shard_map/all_to_all | solution.py:15
  (109 shorter events, 31.0 us)
Async XLA Ops:
  0.6 82.2 %copy-start = (bf16[128,16]{0,1:T(8,128)(2,1)S(1)}, bf16[128,16]{0,1:T(8,128)(2,1)}, u32[]{:S(2)}) copy-start(bf16[128,16]{0,1:T(8,128)(2,1)} %param.13) | copy-start | bytes 12292
  4.3 14.4 %copy-start.9 = (s32[128,2]{0,1:T(2,128)S(1)}, s32[128,2]{0,1:T(2,128)}, u32[]{:S(2)}) copy-start(s32[128,2]{0,1:T(2,128)} %param.14) | copy-start | bytes 3076
  4.3 14.9 %copy-start.7 = (bf16[128,128]{1,0:T(8,128)(2,1)S(1)}, bf16[128,128]{1,0:T(8,128)(2,1)}, u32[]{:S(2)}) copy-start(bf16[128,128]{1,0:T(8,128)(2,1)} %param.9) | copy-start | bytes 98308
  4.4 15.6 %copy-start.10 = (bf16[128]{0:T(256)(128)(2,1)S(1)}, bf16[128]{0:T(256)(128)(2,1)}, u32[]{:S(2)}) copy-start(bf16[128]{0:T(256)(128)(2,1)} %param.12) | copy-start | bytes 772
  6.1 15.1 %copy-start.1 = (bf16[4,1,1408,128]{3,2,1,0:T(8,128)(2,1)S(1)}, bf16[4,1,1408,128]{3,2,1,0:T(8,128)(2,1)}, u32[]{:S(2)}) copy-start(bf16[4,1,1408,128]{3,2,1,0:T(8,128)(2,1)} %get-tuple-element.43) | copy-start | bytes 4325380
  6.1 15.1 %collective-permute-start = (bf16[4,1408,128]{2,1,0:T(8,128)(2,1)}, bf16[4,1408,128]{2,1,0:T(8,128)(2,1)S(1)}, u32[]{:S(2)}, u32[]{:S(2)}) collective-permute-start(bf16[4,1408,128]{2,1,0:T(8,128)(2,1)} %get-tuple-element.42), channel_id=1, source_target_pairs={{0,1},{1,0},{2,3},{3,2},{4,5},{5,4},{6,7},{7,6},{8,9},{9,8},{10,11... | collective-permute-start | bytes 4325384 | tf_op jit(solution)/shard_map/ppermute | solution.py:27
  15.1 37.5 %all-to-all-start = ((bf16[16,128,128]{2,1,0:T(8,128)(2,1)}), bf16[16,128,128]{2,1,0:T(8,128)(2,1)S(1)}, u32[]{:S(2)}, u32[]{:S(2)}) async-start(bf16[16,128,128]{2,1,0:T(8,128)(2,1)} %bitcast.135), calls=%async_computation | async-start | bytes 1048576 | tf_op jit(solution)/shard_map/all_to_all | solution.py:15
  21.2 8.2 %copy-start.8 = (bf16[128,64]{0,1:T(8,128)(2,1)S(1)}, bf16[128,64]{0,1:T(8,128)(2,1)}, u32[]{:S(2)}) copy-start(bf16[128,64]{0,1:T(8,128)(2,1)} %param.10) | copy-start | bytes 49156
  22.9 29.8 %collective-permute-start.1 = (bf16[2,1408,128]{2,1,0:T(8,128)(2,1)}, bf16[2,1408,128]{2,1,0:T(8,128)(2,1)S(1)}, u32[]{:S(2)}, u32[]{:S(2)}) collective-permute-start(bf16[2,1408,128]{2,1,0:T(8,128)(2,1)} %get-tuple-element.39), channel_id=1, source_target_pairs={{0,2},{2,4},{4,6},{6,0},{1,3},{3,5},{5,7},{7,1},{8,10},{10,12},{12... | collective-permute-start | bytes 2162696 | tf_op jit(solution)/shard_map/ppermute | solution.py:27
  25.4 27.3 %collective-permute-start.2 = (bf16[2,1408,128]{2,1,0:T(8,128)(2,1)}, bf16[2,1408,128]{2,1,0:T(8,128)(2,1)S(1)}, u32[]{:S(2)}, u32[]{:S(2)}) collective-permute-start(bf16[2,1408,128]{2,1,0:T(8,128)(2,1)} %get-tuple-element.40), channel_id=1, source_target_pairs={{0,6},{2,0},{4,2},{6,4},{1,7},{3,1},{5,3},{7,5},{8,14},{10,8},{12,... | collective-permute-start | bytes 2162696 | tf_op jit(solution)/shard_map/ppermute | solution.py:27
  49.1 31.7 %collective-permute-start.3 = (bf16[2,1408,128]{2,1,0:T(8,128)(2,1)}, bf16[2,1408,128]{2,1,0:T(8,128)(2,1)}, u32[]{:S(2)}, u32[]{:S(2)}) collective-permute-start(bf16[2,1408,128]{2,1,0:T(8,128)(2,1)} %get-tuple-element.41), channel_id=1, source_target_pairs={{0,4},{2,6},{4,0},{6,2},{1,5},{3,7},{5,1},{7,3},{8,12},{10,14},{12... | collective-permute-start | bytes 2162696 | tf_op jit(solution)/shard_map/ppermute | solution.py:27
  52.6 8.1 %copy-start.4 = (bf16[2,1408,128]{2,1,0:T(8,128)(2,1)}, bf16[2,1408,128]{2,1,0:T(8,128)(2,1)S(1)}, u32[]{:S(2)}) copy-start(bf16[2,1408,128]{2,1,0:T(8,128)(2,1)S(1)} %collective-permute-done.1) | copy-start | bytes 2162692
  52.7 8.1 %copy-start.3 = (bf16[2,1408,128]{2,1,0:T(8,128)(2,1)}, bf16[2,1408,128]{2,1,0:T(8,128)(2,1)S(1)}, u32[]{:S(2)}) copy-start(bf16[2,1408,128]{2,1,0:T(8,128)(2,1)S(1)} %collective-permute-done.2) | copy-start | bytes 2162692
  53.7 27.2 %all-to-all-start.1 = ((bf16[16,128,128]{2,1,0:T(8,128)(2,1)}), bf16[16,128,128]{2,1,0:T(8,128)(2,1)S(1)}, u32[]{:S(2)}, u32[]{:S(2)}) async-start(bf16[16,128,128]{2,1,0:T(8,128)(2,1)} %broadcast_in_dim.19), calls=%async_computation.1 | async-start | bytes 1048576 | tf_op jit(solution)/shard_map/all_to_all | solution.py:15
  60.8 1.3 copy-start.5
  84.7 15.2 %all-to-all-start.2 = ((bf16[16,25,128]{2,1,0:T(8,128)(2,1)}), bf16[16,25,128]{2,1,0:T(8,128)(2,1)S(1)}, u32[]{:S(2)}, u32[]{:S(2)}) async-start(bf16[16,25,128]{2,1,0:T(8,128)(2,1)} %fusion.33), calls=%async_computation.2 | async-start | bytes 262144 | tf_op jit(solution)/shard_map/all_to_all | solution.py:15
  117.8 32.6 %collective-permute-start.4 = (bf16[368,384]{1,0:T(8,128)(2,1)S(1)}, bf16[368,384]{1,0:T(8,128)(2,1)}, u32[]{:S(2)}, u32[]{:S(2)}) collective-permute-start(bf16[368,384]{1,0:T(8,128)(2,1)S(1)} %pad_maximum_fusion), channel_id=1, source_target_pairs={{0,24},{8,0},{16,8},{24,16},{1,25},{9,1},{17,9},{25,17},{2,26},{10... | collective-permute-start | bytes 847880 | tf_op jit(solution)/shard_map/ppermute | solution.py:27
  121.9 33.5 %collective-permute-start.5 = (bf16[368,384]{1,0:T(8,128)(2,1)S(1)}, bf16[368,384]{1,0:T(8,128)(2,1)}, u32[]{:S(2)}, u32[]{:S(2)}) collective-permute-start(bf16[368,384]{1,0:T(8,128)(2,1)S(1)} %pad_maximum_fusion.1), channel_id=1, source_target_pairs={{0,8},{8,16},{16,24},{24,0},{1,9},{9,17},{17,25},{25,1},{2,10},{10... | collective-permute-start | bytes 847880 | tf_op jit(solution)/shard_map/ppermute | solution.py:27
  127.1 67.4 %all-to-all-start.3 = ((bf16[8,704,128]{2,1,0:T(8,128)(2,1)}), bf16[8,704,128]{2,1,0:T(8,128)(2,1)S(1)}, u32[]{:S(2)}, u32[]{:S(2)}) async-start(bf16[8,704,128]{2,1,0:T(8,128)(2,1)} %bitcast.43), calls=%async_computation.3 | async-start | bytes 2883584 | tf_op jit(solution)/shard_map/all_to_all | solution.py:15
  151.4 13.1 %collective-permute-start.7 = (bf16[192,384]{1,0:T(8,128)(2,1)S(1)}, bf16[192,384]{1,0:T(8,128)(2,1)S(1)}, u32[]{:S(2)}, u32[]{:S(2)}) collective-permute-start(bf16[192,384]{1,0:T(8,128)(2,1)S(1)} %fusion.16), channel_id=1, source_target_pairs={{0,24},{8,0},{16,8},{24,16},{1,25},{9,1},{17,9},{25,17},{2,26},{10... | collective-permute-start | bytes 442376 | tf_op jit(solution)/shard_map/ppermute | solution.py:27
  156.3 14.1 %collective-permute-start.6 = (bf16[176,384]{1,0:T(8,128)(2,1)S(1)}, bf16[176,384]{1,0:T(8,128)(2,1)S(1)}, u32[]{:S(2)}, u32[]{:S(2)}) collective-permute-start(bf16[176,384]{1,0:T(8,128)(2,1)S(1)} %fusion.20), channel_id=1, source_target_pairs={{0,8},{8,16},{16,24},{24,0},{1,9},{9,17},{17,25},{25,1},{2,10},{10... | collective-permute-start | bytes 405512 | tf_op jit(solution)/shard_map/ppermute | solution.py:27
  196.1 22.9 %copy-start.6 = (bf16[128,128]{0,1:T(8,128)(2,1)S(1)}, bf16[128,128]{0,1:T(8,128)(2,1)}, u32[]{:S(2)}) copy-start(bf16[128,128]{0,1:T(8,128)(2,1)} %get-tuple-element.51) | copy-start | bytes 98308
  196.1 17.0 %all-to-all-start.4 = ((bf16[8,384,128]{2,1,0:T(8,128)(2,1)}), bf16[8,384,128]{2,1,0:T(8,128)(2,1)S(1)}, u32[]{:S(2)}, u32[]{:S(2)}) async-start(bf16[8,384,128]{2,1,0:T(8,128)(2,1)} %fusion.4), calls=%async_computation.4 | async-start | bytes 1572864 | tf_op jit(solution)/shard_map/all_to_all | solution.py:15
  214.0 12.7 %all-to-all-start.5 = ((bf16[16,24,128]{2,1,0:T(8,128)(2,1)}), bf16[16,24,128]{2,1,0:T(8,128)(2,1)S(1)}, u32[]{:S(2)}, u32[]{:S(2)}) async-start(bf16[16,24,128]{2,1,0:T(8,128)(2,1)} %multiply_convert_fusion), calls=%async_computation.5 | async-start | bytes 196608 | tf_op jit(solution)/shard_map/all_to_all | solution.py:15
  (1 other events, 1.1 us)

commit v3 on v2

--- a/solution.py
+++ b/solution.py
@@ -73,15 +73,6 @@
 def relay_x(both):
     x = lax.axis_index("x")
     return [at(both, x)] + [shift(at(both, (x + k) % 4), "x", k, 4) for k in (1, 2, 3)]
-
-
-def gather_far(values):
-    z = lax.axis_index("zh")
-    held = jnp.zeros((4,) + values.shape, values.dtype)
-    for k in range(4):
-        came = shift(values, "zh", k, 4) if k else values
-        held = lax.dynamic_update_index_in_dim(held, came, (z + 4 - k) % 4, 0)
-    return held
 
 
 def sum_far(gate, up):
@@ -103,9 +94,12 @@
 
 def group_slots(group_routes, experts):
     flat = group_routes.reshape(-1)
-    onehot = (flat[:, None] == jnp.arange(experts, dtype=jnp.int32)[None, :]).astype(jnp.int32)
-    before = jnp.cumsum(onehot, axis=0) - onehot
-    return jnp.sum(before * onehot, axis=1).reshape(group_routes.shape)
+    pairs = jnp.arange(flat.shape[0], dtype=jnp.int32)
+    onehot = (flat[:, None] == jnp.arange(experts, dtype=jnp.int32)[None, :]).astype(BF)
+    earlier = (pairs[:, None] > pairs[None, :]).astype(BF)
+    before = jnp.dot(earlier, onehot, preferred_element_type=F32)
+    slots = jnp.sum(before * onehot.astype(F32), axis=1)
+    return slots.astype(jnp.int32).reshape(group_routes.shape)
 
 
 def body(tokens, context, attn_weights, norm_gain, router, routes, gate_w, up_w, down_w):
@@ -162,7 +156,7 @@
     extra = jnp.sum(near[:, rows:, : 4 * capacity].astype(F32), axis=0)
     extra = extra.reshape(experts, 4, capacity).transpose(1, 0, 2).reshape(4, rows)
     extra_high, extra_low = halves(jnp.stack([extra[0] + extra[1], extra[2] + extra[3]]))
-    extra = jnp.concatenate([extra_high, extra_low, jnp.zeros((12, rows), BF)])
+    extra = jnp.concatenate([extra_high, extra_low, jnp.zeros((4, rows), BF)])
 
     down_blocks, near = lax.optimization_barrier((down_w[0], near))
     down_r = swap(down_blocks.reshape(8, near_units, width), NEAR)
@@ -171,7 +165,7 @@
         weights, near, (((0, 2), (0, 2)), ((), ())), preferred_element_type=F32
     )
     product = product[:, :rows].astype(BF).reshape(2, 4, own_units, rows)
-    extra = jnp.broadcast_to(extra[None], (4, 16, rows))
+    extra = jnp.broadcast_to(extra[None], (4, 8, rows))
     gate, up = sum_far(product[0], jnp.concatenate([product[1], extra], axis=1))
     square_sum = up[own_units] + up[own_units + 2]
     score = up[own_units + 1] + up[own_units + 3]

time: 229 us -> 228 us (level)
  transfers between devices with their start and end apart: 14 -> 14, of which waited for: 6 -> 7; matrix products, arithmetic and copies ran while one was open for 6% -> 6% of each run, Pallas kernels for 0% -> 0%
where the time goes in v3:
time: 228 us; the launch traced here: 227 us
  blocking collectives  77.2 us (34%)
  starting transfers between devices  69.1 us (30%)
  waiting for transfers between devices  49.6 us (22%)
  local copies, waits for them, and re-layouts  13.6 us (6%)
  other arithmetic  9.31 us (4%)
  matrix products  7 us (3%)
    ppermute x8, starting transfers between devices, shift(): lax.ppermute(values, axis, [(i, (i + step) % count) for i in range(count)])  36.9 us
    all_to_all x6, starting transfers between devices, swap(): lax.all_to_all(values, axes, split_axis=0, concat_axis=0, tiled=False)  32.2 us
    ppermute x8, waiting for transfers between devices, shift(): lax.ppermute(values, axis, [(i, (i + step) % count) for i in range(count)])  26.7 us
    all_gather x1, blocking collectives, body(): hidden = lax.all_gather(hidden, 'zh', axis=0, tiled=True)  23.9 us
    all_to_all x6, waiting for transfers between devices, swap(): lax.all_to_all(values, axes, split_axis=0, concat_axis=0, tiled=False)  22.9 us
    all_gather x1, blocking collectives, body(): ctx = lax.all_gather(context.T, 'zh', axis=0, tiled=False)  19.7 us
    all_gather x1, blocking collectives, body(): lax.all_gather(ctx, NEAR, axis=1, tiled=False).reshape(heads, token_count)  18.6 us
    all_gather x1, blocking collectives, body(): near = lax.all_gather(received, NEAR, axis=0, tiled=False)  15 us
  transfers between devices with their start and end apart: 14, of which 7 were waited for; matrix products, arithmetic and copies ran while one was open for 6% of the time, Pallas kernels for 0%

profile of v3, /device:TPU:1, one launch (start us, length us, event | category | flops | bytes accessed | tf_op | source)
XLA Modules:
  0.0 227.2 jit_solution(739161332023810043)
XLA Ops:
  6.1 8.8 %collective-permute-start = (bf16[4,1408,128]{2,1,0:T(8,128)(2,1)}, bf16[4,1408,128]{2,1,0:T(8,128)(2,1)S(1)}, u32[]{:S(2)}, u32[]{:S(2)}) collective-permute-start(bf16[4,1408,128]{2,1,0:T(8,128)(2,1)} %get-tuple-element.42), channel_id=1, source_target_pairs={{0,1},{1,0},{2,3},{3,2},{4,5},{5,4},{6,7},{7,6},{8,9},{9,8},{10,11... | collective-permute-start | bytes 4325384 | tf_op jit(solution)/shard_map/ppermute | solution.py:27
  14.9 3.6 %all-to-all-start = ((bf16[16,128,128]{2,1,0:T(8,128)(2,1)}), bf16[16,128,128]{2,1,0:T(8,128)(2,1)S(1)}, u32[]{:S(2)}, u32[]{:S(2)}) async-start(bf16[16,128,128]{2,1,0:T(8,128)(2,1)} %bitcast.117), calls=%async_computation | async-start | bytes 1048576 | tf_op jit(solution)/shard_map/all_to_all | solution.py:15
  20.2 2.7 %fusion.6 = (bf16[1,2,1408,128]{3,2,1,0:T(8,128)(2,1)}, bf16[2,1408,128]{2,1,0:T(8,128)(2,1)S(1)}, bf16[2,1408,128]{2,1,0:T(8,128)(2,1)S(1)}, bf16[2,1408,128]{2,1,0:T(8,128)(2,1)}) fusion(s32[]{:T(128)S(6)} %select_n.148, bf16[4,1,1408,128]{3,2,1,0:T(8,128)(2,1)} %get-tuple-element.43, bf16[4,1,1408,128]{3,2,1,0:T(8,128)(2,1)S(1)} %bitcast.113, ...), kind=kLoop, calls=%fused_computation.30 | loop fusion | flops 1441792 | bytes 5767184 | tf_op jit(solution)/shard_map/stack | solution.py:70
  25.5 4.0 %collective-permute-start.2 = (bf16[2,1408,128]{2,1,0:T(8,128)(2,1)S(1)}, bf16[2,1408,128]{2,1,0:T(8,128)(2,1)S(1)}, u32[]{:S(2)}, u32[]{:S(2)}) collective-permute-start(bf16[2,1408,128]{2,1,0:T(8,128)(2,1)S(1)} %get-tuple-element.40), channel_id=1, source_target_pairs={{0,6},{2,0},{4,2},{6,4},{1,7},{3,1},{5,3},{7,5},{8,14},{10,8},{12,... | collective-permute-start | bytes 2162696 | tf_op jit(solution)/shard_map/ppermute | solution.py:27
  29.4 19.7 %all-gather = bf16[256,128]{1,0:T(8,128)(2,1)S(1)} all-gather(bf16[64,128]{1,0:T(8,128)(2,1)S(1)} %bitcast.125), channel_id=2, replica_groups=mesh['zl'=4,'y'=4,'zh'=4,'x'=4,'c'=2] {'zh'}, dimensions={0}, use_global_device_ids=true | all-gather | bytes 81920 | tf_op jit(solution)/shard_map/all_gather | solution.py:127
  49.2 3.4 %collective-permute-start.3 = (bf16[2,1408,128]{2,1,0:T(8,128)(2,1)}, bf16[2,1408,128]{2,1,0:T(8,128)(2,1)}, u32[]{:S(2)}, u32[]{:S(2)}) collective-permute-start(bf16[2,1408,128]{2,1,0:T(8,128)(2,1)} %get-tuple-element.41), channel_id=1, source_target_pairs={{0,4},{2,6},{4,0},{6,2},{1,5},{3,7},{5,1},{7,3},{8,12},{10,14},{12... | collective-permute-start | bytes 2162696 | tf_op jit(solution)/shard_map/ppermute | solution.py:27
  53.8 7.0 %all-to-all-start.1 = ((bf16[16,128,128]{2,1,0:T(8,128)(2,1)}), bf16[16,128,128]{2,1,0:T(8,128)(2,1)S(1)}, u32[]{:S(2)}, u32[]{:S(2)}) async-start(bf16[16,128,128]{2,1,0:T(8,128)(2,1)} %broadcast_in_dim.19), calls=%async_computation.1 | async-start | bytes 1048576 | tf_op jit(solution)/shard_map/all_to_all | solution.py:15
  62.2 18.6 %all-gather.1 = bf16[4,512,128]{2,1,0:T(8,128)(2,1)} all-gather(bf16[4,64,128]{2,1,0:T(8,128)(2,1)S(1)} %bitcast.121), channel_id=3, replica_groups=mesh['zl'=4,'y'=4,'zh'=4,'x'=4,'c'=2] {'x','c'}, dimensions={1}, use_global_device_ids=true | all-gather | bytes 589824 | tf_op jit(solution)/shard_map/all_gather | solution.py:132
  84.7 7.2 %all-to-all-start.2 = ((bf16[16,25,128]{2,1,0:T(8,128)(2,1)}), bf16[16,25,128]{2,1,0:T(8,128)(2,1)S(1)}, u32[]{:S(2)}, u32[]{:S(2)}) async-start(bf16[16,25,128]{2,1,0:T(8,128)(2,1)} %fusion.34), calls=%async_computation.2 | async-start | bytes 262144 | tf_op jit(solution)/shard_map/all_to_all | solution.py:15
  96.1 3.8 %all-to-all-done.2 = bf16[16,25,128]{2,1,0:T(8,128)(2,1)S(1)} async-done(((bf16[16,25,128]{2,1,0:T(8,128)(2,1)}), bf16[16,25,128]{2,1,0:T(8,128)(2,1)S(1)}, u32[]{:S(2)}, u32[]{:S(2)}) %all-to-all-start.2) | async-done | bytes 102432 | tf_op jit(solution)/shard_map/all_to_all | solution.py:15
  100.0 15.0 %all-gather.2 = bf16[3200,128]{1,0:T(8,128)(2,1)S(1)} all-gather(bf16[400,128]{1,0:T(8,128)(2,1)S(1)} %pad_maximum_fusion.2), channel_id=4, replica_groups=mesh['zl'=4,'y'=4,'zh'=4,'x'=4,'c'=2] {'x','c'}, dimensions={0}, use_global_device_ids=true | all-gather | bytes 921600 | tf_op jit(solution)/shard_map/all_gather | solution.py:155
  118.5 4.0 %collective-permute-start.4 = (bf16[360,384]{1,0:T(8,128)(2,1)}, bf16[360,384]{1,0:T(8,128)(2,1)S(1)}, u32[]{:S(2)}, u32[]{:S(2)}) collective-permute-start(bf16[360,384]{1,0:T(8,128)(2,1)} %pad_maximum_fusion), channel_id=1, source_target_pairs={{0,24},{8,0},{16,8},{24,16},{1,25},{9,1},{17,9},{25,17},{2,26},{10... | collective-permute-start | bytes 829448 | tf_op jit(solution)/shard_map/ppermute | solution.py:27
  123.3 5.1 %collective-permute-start.5 = (bf16[360,384]{1,0:T(8,128)(2,1)}, bf16[360,384]{1,0:T(8,128)(2,1)S(1)}, u32[]{:S(2)}, u32[]{:S(2)}) collective-permute-start(bf16[360,384]{1,0:T(8,128)(2,1)} %pad_maximum_fusion.1), channel_id=1, source_target_pairs={{0,8},{8,16},{16,24},{24,0},{1,9},{9,17},{17,25},{25,1},{2,10},{10... | collective-permute-start | bytes 829448 | tf_op jit(solution)/shard_map/ppermute | solution.py:27
  128.4 4.2 %all-to-all-start.3 = ((bf16[8,704,128]{2,1,0:T(8,128)(2,1)}), bf16[8,704,128]{2,1,0:T(8,128)(2,1)S(1)}, u32[]{:S(2)}, u32[]{:S(2)}) async-start(bf16[8,704,128]{2,1,0:T(8,128)(2,1)} %bitcast.112), calls=%async_computation.3 | async-start | bytes 2883584 | tf_op jit(solution)/shard_map/all_to_all | solution.py:15
  132.7 18.0 %collective-permute-done.4 = bf16[360,384]{1,0:T(8,128)(2,1)S(1)} collective-permute-done((bf16[360,384]{1,0:T(8,128)(2,1)}, bf16[360,384]{1,0:T(8,128)(2,1)S(1)}, u32[]{:S(2)}, u32[]{:S(2)}) %collective-permute-start.4) | collective-permute-done | bytes 276512 | tf_op jit(solution)/shard_map/ppermute | solution.py:27
  150.7 4.0 %collective-permute-start.7 = (bf16[184,384]{1,0:T(8,128)(2,1)S(1)}, bf16[184,384]{1,0:T(8,128)(2,1)S(1)}, u32[]{:S(2)}, u32[]{:S(2)}) collective-permute-start(bf16[184,384]{1,0:T(8,128)(2,1)S(1)} %fusion.17), channel_id=1, source_target_pairs={{0,24},{8,0},{16,8},{24,16},{1,25},{9,1},{17,9},{25,17},{2,26},{10... | collective-permute-start | bytes 423944 | tf_op jit(solution)/shard_map/ppermute | solution.py:27
  155.4 5.1 %collective-permute-start.6 = (bf16[176,384]{1,0:T(8,128)(2,1)S(1)}, bf16[176,384]{1,0:T(8,128)(2,1)S(1)}, u32[]{:S(2)}, u32[]{:S(2)}) collective-permute-start(bf16[176,384]{1,0:T(8,128)(2,1)S(1)} %fusion.21), channel_id=1, source_target_pairs={{0,8},{8,16},{16,24},{24,0},{1,9},{9,17},{17,25},{25,1},{2,10},{10... | collective-permute-start | bytes 405512 | tf_op jit(solution)/shard_map/ppermute | solution.py:27
  160.5 3.9 %collective-permute-done.7 = bf16[184,384]{1,0:T(8,128)(2,1)S(1)} collective-permute-done((bf16[184,384]{1,0:T(8,128)(2,1)S(1)}, bf16[184,384]{1,0:T(8,128)(2,1)S(1)}, u32[]{:S(2)}, u32[]{:S(2)}) %collective-permute-start.7) | collective-permute-done | bytes 141344 | tf_op jit(solution)/shard_map/ppermute | solution.py:27
  165.4 4.2 %collective-permute-done.6 = bf16[176,384]{1,0:T(8,128)(2,1)S(1)} collective-permute-done((bf16[176,384]{1,0:T(8,128)(2,1)S(1)}, bf16[176,384]{1,0:T(8,128)(2,1)S(1)}, u32[]{:S(2)}, u32[]{:S(2)}) %collective-permute-start.6) | collective-permute-done | bytes 135200 | tf_op jit(solution)/shard_map/ppermute | solution.py:27
  169.7 23.9 %all_gather.27 = bf16[704,384]{1,0:T(8,128)(2,1)S(1)} all-gather(bf16[176,384]{1,0:T(8,128)(2,1)S(1)} %fusion.20), channel_id=1, replica_groups=mesh['zl'=4,'y'=4,'zh'=4,'x'=4,'c'=2] {'zh'}, dimensions={0}, use_global_device_ids=true | all-gather | bytes 675840 | tf_op jit(solution)/shard_map/all_gather | solution.py:177
  195.3 4.2 %all-to-all-start.4 = ((bf16[8,384,128]{2,1,0:T(8,128)(2,1)}), bf16[8,384,128]{2,1,0:T(8,128)(2,1)S(1)}, u32[]{:S(2)}, u32[]{:S(2)}) async-start(bf16[8,384,128]{2,1,0:T(8,128)(2,1)} %fusion.4), calls=%async_computation.4 | async-start | bytes 1572864 | tf_op jit(solution)/shard_map/all_to_all | solution.py:15
  199.6 12.2 %all-to-all-done.4 = bf16[8,384,128]{2,1,0:T(8,128)(2,1)S(1)} async-done(((bf16[8,384,128]{2,1,0:T(8,128)(2,1)}), bf16[8,384,128]{2,1,0:T(8,128)(2,1)S(1)}, u32[]{:S(2)}, u32[]{:S(2)}) %all-to-all-start.4) | async-done | bytes 786464 | tf_op jit(solution)/shard_map/all_to_all | solution.py:15
  212.7 6.0 %all-to-all-start.5 = ((bf16[16,24,128]{2,1,0:T(8,128)(2,1)}), bf16[16,24,128]{2,1,0:T(8,128)(2,1)S(1)}, u32[]{:S(2)}, u32[]{:S(2)}) async-start(bf16[16,24,128]{2,1,0:T(8,128)(2,1)} %multiply_convert_fusion), calls=%async_computation.5 | async-start | bytes 196608 | tf_op jit(solution)/shard_map/all_to_all | solution.py:15
  219.4 6.9 %all-to-all-done.5 = bf16[16,24,128]{2,1,0:T(8,128)(2,1)S(1)} async-done(((bf16[16,24,128]{2,1,0:T(8,128)(2,1)}), bf16[16,24,128]{2,1,0:T(8,128)(2,1)S(1)}, u32[]{:S(2)}, u32[]{:S(2)}) %all-to-all-start.5) | async-done | bytes 98336 | tf_op jit(solution)/shard_map/all_to_all | solution.py:15
  (104 shorter events, 30.3 us)
Async XLA Ops:
  0.6 82.3 %copy-start = (bf16[128,16]{0,1:T(8,128)(2,1)S(1)}, bf16[128,16]{0,1:T(8,128)(2,1)}, u32[]{:S(2)}) copy-start(bf16[128,16]{0,1:T(8,128)(2,1)} %param.13) | copy-start | bytes 12292
  4.3 14.3 %copy-start.7 = (bf16[128,128]{1,0:T(8,128)(2,1)S(1)}, bf16[128,128]{1,0:T(8,128)(2,1)}, u32[]{:S(2)}) copy-start(bf16[128,128]{1,0:T(8,128)(2,1)} %param.9) | copy-start | bytes 98308
  4.3 15.1 %copy-start.10 = (bf16[128]{0:T(256)(128)(2,1)S(1)}, bf16[128]{0:T(256)(128)(2,1)}, u32[]{:S(2)}) copy-start(bf16[128]{0:T(256)(128)(2,1)} %param.12) | copy-start | bytes 772
  4.4 15.1 %copy-start.9 = (s32[128,2]{0,1:T(2,128)S(1)}, s32[128,2]{0,1:T(2,128)}, u32[]{:S(2)}) copy-start(s32[128,2]{0,1:T(2,128)} %param.14) | copy-start | bytes 3076
  6.1 14.1 %collective-permute-start = (bf16[4,1408,128]{2,1,0:T(8,128)(2,1)}, bf16[4,1408,128]{2,1,0:T(8,128)(2,1)S(1)}, u32[]{:S(2)}, u32[]{:S(2)}) collective-permute-start(bf16[4,1408,128]{2,1,0:T(8,128)(2,1)} %get-tuple-element.42), channel_id=1, source_target_pairs={{0,1},{1,0},{2,3},{3,2},{4,5},{5,4},{6,7},{7,6},{8,9},{9,8},{10,11... | collective-permute-start | bytes 4325384 | tf_op jit(solution)/shard_map/ppermute | solution.py:27
  14.9 37.7 %all-to-all-start = ((bf16[16,128,128]{2,1,0:T(8,128)(2,1)}), bf16[16,128,128]{2,1,0:T(8,128)(2,1)S(1)}, u32[]{:S(2)}, u32[]{:S(2)}) async-start(bf16[16,128,128]{2,1,0:T(8,128)(2,1)} %bitcast.117), calls=%async_computation | async-start | bytes 1048576 | tf_op jit(solution)/shard_map/all_to_all | solution.py:15
  20.2 9.2 %copy-start.8 = (bf16[128,64]{0,1:T(8,128)(2,1)S(1)}, bf16[128,64]{0,1:T(8,128)(2,1)}, u32[]{:S(2)}) copy-start(bf16[128,64]{0,1:T(8,128)(2,1)} %param.10) | copy-start | bytes 49156
  22.9 29.8 %collective-permute-start.1 = (bf16[2,1408,128]{2,1,0:T(8,128)(2,1)S(1)}, bf16[2,1408,128]{2,1,0:T(8,128)(2,1)S(1)}, u32[]{:S(2)}, u32[]{:S(2)}) collective-permute-start(bf16[2,1408,128]{2,1,0:T(8,128)(2,1)S(1)} %get-tuple-element.39), channel_id=1, source_target_pairs={{0,2},{2,4},{4,6},{6,0},{1,3},{3,5},{5,7},{7,1},{8,10},{10,12},{12... | collective-permute-start | bytes 2162696 | tf_op jit(solution)/shard_map/ppermute | solution.py:27
  25.5 27.3 %collective-permute-start.2 = (bf16[2,1408,128]{2,1,0:T(8,128)(2,1)S(1)}, bf16[2,1408,128]{2,1,0:T(8,128)(2,1)S(1)}, u32[]{:S(2)}, u32[]{:S(2)}) collective-permute-start(bf16[2,1408,128]{2,1,0:T(8,128)(2,1)S(1)} %get-tuple-element.40), channel_id=1, source_target_pairs={{0,6},{2,0},{4,2},{6,4},{1,7},{3,1},{5,3},{7,5},{8,14},{10,8},{12,... | collective-permute-start | bytes 2162696 | tf_op jit(solution)/shard_map/ppermute | solution.py:27
  49.2 31.7 %collective-permute-start.3 = (bf16[2,1408,128]{2,1,0:T(8,128)(2,1)}, bf16[2,1408,128]{2,1,0:T(8,128)(2,1)}, u32[]{:S(2)}, u32[]{:S(2)}) collective-permute-start(bf16[2,1408,128]{2,1,0:T(8,128)(2,1)} %get-tuple-element.41), channel_id=1, source_target_pairs={{0,4},{2,6},{4,0},{6,2},{1,5},{3,7},{5,1},{7,3},{8,12},{10,14},{12... | collective-permute-start | bytes 2162696 | tf_op jit(solution)/shard_map/ppermute | solution.py:27
  52.7 8.0 %copy-start.3 = (bf16[2,1408,128]{2,1,0:T(8,128)(2,1)}, bf16[2,1408,128]{2,1,0:T(8,128)(2,1)S(1)}, u32[]{:S(2)}) copy-start(bf16[2,1408,128]{2,1,0:T(8,128)(2,1)S(1)} %collective-permute-done.1) | copy-start | bytes 2162692
  52.8 8.0 %copy-start.2 = (bf16[2,1408,128]{2,1,0:T(8,128)(2,1)}, bf16[2,1408,128]{2,1,0:T(8,128)(2,1)S(1)}, u32[]{:S(2)}) copy-start(bf16[2,1408,128]{2,1,0:T(8,128)(2,1)S(1)} %collective-permute-done.2) | copy-start | bytes 2162692
  53.8 27.1 %all-to-all-start.1 = ((bf16[16,128,128]{2,1,0:T(8,128)(2,1)}), bf16[16,128,128]{2,1,0:T(8,128)(2,1)S(1)}, u32[]{:S(2)}, u32[]{:S(2)}) async-start(bf16[16,128,128]{2,1,0:T(8,128)(2,1)} %broadcast_in_dim.19), calls=%async_computation.1 | async-start | bytes 1048576 | tf_op jit(solution)/shard_map/all_to_all | solution.py:15
  60.8 1.3 copy-start.4
  84.7 15.2 %all-to-all-start.2 = ((bf16[16,25,128]{2,1,0:T(8,128)(2,1)}), bf16[16,25,128]{2,1,0:T(8,128)(2,1)S(1)}, u32[]{:S(2)}, u32[]{:S(2)}) async-start(bf16[16,25,128]{2,1,0:T(8,128)(2,1)} %fusion.34), calls=%async_computation.2 | async-start | bytes 262144 | tf_op jit(solution)/shard_map/all_to_all | solution.py:15
  118.5 32.2 %collective-permute-start.4 = (bf16[360,384]{1,0:T(8,128)(2,1)}, bf16[360,384]{1,0:T(8,128)(2,1)S(1)}, u32[]{:S(2)}, u32[]{:S(2)}) collective-permute-start(bf16[360,384]{1,0:T(8,128)(2,1)} %pad_maximum_fusion), channel_id=1, source_target_pairs={{0,24},{8,0},{16,8},{24,16},{1,25},{9,1},{17,9},{25,17},{2,26},{10... | collective-permute-start | bytes 829448 | tf_op jit(solution)/shard_map/ppermute | solution.py:27
  123.3 32.0 %collective-permute-start.5 = (bf16[360,384]{1,0:T(8,128)(2,1)}, bf16[360,384]{1,0:T(8,128)(2,1)S(1)}, u32[]{:S(2)}, u32[]{:S(2)}) collective-permute-start(bf16[360,384]{1,0:T(8,128)(2,1)} %pad_maximum_fusion.1), channel_id=1, source_target_pairs={{0,8},{8,16},{16,24},{24,0},{1,9},{9,17},{17,25},{25,1},{2,10},{10... | collective-permute-start | bytes 829448 | tf_op jit(solution)/shard_map/ppermute | solution.py:27
  128.4 65.2 %all-to-all-start.3 = ((bf16[8,704,128]{2,1,0:T(8,128)(2,1)}), bf16[8,704,128]{2,1,0:T(8,128)(2,1)S(1)}, u32[]{:S(2)}, u32[]{:S(2)}) async-start(bf16[8,704,128]{2,1,0:T(8,128)(2,1)} %bitcast.112), calls=%async_computation.3 | async-start | bytes 2883584 | tf_op jit(solution)/shard_map/all_to_all | solution.py:15
  150.7 13.6 %collective-permute-start.7 = (bf16[184,384]{1,0:T(8,128)(2,1)S(1)}, bf16[184,384]{1,0:T(8,128)(2,1)S(1)}, u32[]{:S(2)}, u32[]{:S(2)}) collective-permute-start(bf16[184,384]{1,0:T(8,128)(2,1)S(1)} %fusion.17), channel_id=1, source_target_pairs={{0,24},{8,0},{16,8},{24,16},{1,25},{9,1},{17,9},{25,17},{2,26},{10... | collective-permute-start | bytes 423944 | tf_op jit(solution)/shard_map/ppermute | solution.py:27
  155.3 5.1 %copy-start.5 = (bf16[360,384]{1,0:T(8,128)(2,1)}, bf16[360,384]{1,0:T(8,128)(2,1)S(1)}, u32[]{:S(2)}) copy-start(bf16[360,384]{1,0:T(8,128)(2,1)S(1)} %collective-permute-done.5) | copy-start | bytes 829444
  155.4 14.2 %collective-permute-start.6 = (bf16[176,384]{1,0:T(8,128)(2,1)S(1)}, bf16[176,384]{1,0:T(8,128)(2,1)S(1)}, u32[]{:S(2)}, u32[]{:S(2)}) collective-permute-start(bf16[176,384]{1,0:T(8,128)(2,1)S(1)} %fusion.21), channel_id=1, source_target_pairs={{0,8},{8,16},{16,24},{24,0},{1,9},{9,17},{17,25},{25,1},{2,10},{10... | collective-permute-start | bytes 405512 | tf_op jit(solution)/shard_map/ppermute | solution.py:27
  195.3 23.4 %copy-start.6 = (bf16[128,128]{0,1:T(8,128)(2,1)S(1)}, bf16[128,128]{0,1:T(8,128)(2,1)}, u32[]{:S(2)}) copy-start(bf16[128,128]{0,1:T(8,128)(2,1)} %get-tuple-element.51) | copy-start | bytes 98308
  195.3 16.5 %all-to-all-start.4 = ((bf16[8,384,128]{2,1,0:T(8,128)(2,1)}), bf16[8,384,128]{2,1,0:T(8,128)(2,1)S(1)}, u32[]{:S(2)}, u32[]{:S(2)}) async-start(bf16[8,384,128]{2,1,0:T(8,128)(2,1)} %fusion.4), calls=%async_computation.4 | async-start | bytes 1572864 | tf_op jit(solution)/shard_map/all_to_all | solution.py:15
  212.7 13.7 %all-to-all-start.5 = ((bf16[16,24,128]{2,1,0:T(8,128)(2,1)}), bf16[16,24,128]{2,1,0:T(8,128)(2,1)S(1)}, u32[]{:S(2)}, u32[]{:S(2)}) async-start(bf16[16,24,128]{2,1,0:T(8,128)(2,1)} %multiply_convert_fusion), calls=%async_computation.5 | async-start | bytes 196608 | tf_op jit(solution)/shard_map/all_to_all | solution.py:15
  (1 other events, 1.1 us)

commit v4 on v3

--- a/solution.py
+++ b/solution.py
@@ -56,35 +56,20 @@
     return held
 
 
-def add(*terms):
-    total = terms[0].astype(F32)
-    for term in terms[1:]:
-        total = total + term.astype(F32)
-    return total
-
-
-def pair_up(blocks):
-    core = lax.axis_index("c")
-    kept = lax.dynamic_index_in_dim(blocks, core, 1, keepdims=False)
-    other = lax.dynamic_index_in_dim(blocks, 1 - core, 1, keepdims=False)
-    return jnp.stack([kept, shift(other, "c", 1, 2)], axis=1)
-
-
-def relay_x(both):
-    x = lax.axis_index("x")
-    return [at(both, x)] + [shift(at(both, (x + k) % 4), "x", k, 4) for k in (1, 2, 3)]
+def shift_far(values, step):
+    pairs = [(2 * z + c, 2 * ((z + step * (1 - 2 * c)) % 4) + c) for z in range(4) for c in range(2)]
+    return lax.ppermute(values, ("zh", "c"), pairs)
 
 
 def sum_far(gate, up):
-    z = lax.axis_index("zh")
-    g = [at(gate, (z + k) % 4) for k in range(4)]
-    u = [at(up, (z + k) % 4) for k in range(4)]
+    z, turn = lax.axis_index("zh"), 1 + 2 * lax.axis_index("c")
+    g = [at(gate, (z + turn * k) % 4) for k in range(4)]
+    u = [at(up, (z + turn * k) % 4) for k in range(4)]
     n, m = g[0].shape[0], u[0].shape[0]
-    ahead = shift(jnp.concatenate([g[2], u[1]]), "zh", 1, 4)
-    back = shift(jnp.concatenate([u[2], g[3]]), "zh", 3, 4)
-    ahead_two = shift(add(g[1], ahead[:n]).astype(BF), "zh", 1, 4)
-    back_two = shift(add(u[3], back[:m]).astype(BF), "zh", 3, 4)
-    return add(g[0], back[m:], ahead_two), add(u[0], ahead[n:], back_two)
+    first, second = shift_far(g[2], 1), shift_far(u[2], -1)
+    ahead = shift_far(jnp.concatenate([add(g[1], first).astype(BF), u[1]]), 1)
+    back = shift_far(jnp.concatenate([add(u[3], second).astype(BF), g[3]]), -1)
+    return add(g[0], back[m:], ahead[:n]), add(u[0], ahead[n:], back[:m])
 
 
 def halves(values):

time: 228 us -> 224 us (0.982)
  waiting for transfers between devices: 49.6 us -> 42.3 us
    ppermute x8 -> x4, waiting for transfers between devices: 26.7 us -> 0.01 us  [shift(): lax.ppermute(values, axis, [(i, (i + step) % count) for i in range(count)])]
    ppermute x0 -> x4, waiting for transfers between devices: none -> 19.4 us  [shift_far(): return lax.ppermute(values, ('zh', 'c'), pairs)]
    ppermute x8 -> x4, starting transfers between devices: 36.9 us -> 18.7 us  [shift(): lax.ppermute(values, axis, [(i, (i + step) % count) for i in range(count)])]
    ppermute x0 -> x4, starting transfers between devices: none -> 17.9 us  [shift_far(): return lax.ppermute(values, ('zh', 'c'), pairs)]
    unnamed x28 -> x26, local copies, waits for them, and re-layouts: 6.09 us -> 6.09 us
  transfers between devices with their start and end apart: 14 -> 14, of which waited for: 7 -> 6; matrix products, arithmetic and copies ran while one was open for 6% -> 7% of each run, Pallas kernels for 0% -> 0%
where the time goes in v4:
time: 224 us; the launch traced here: 223 us
  blocking collectives  77.9 us (35%)
  starting transfers between devices  70 us (31%)
  waiting for transfers between devices  42.3 us (19%)
  local copies, waits for them, and re-layouts  13.6 us (6%)
  other arithmetic  10.5 us (5%)
  matrix products  7 us (3%)
    all_to_all x6, starting transfers between devices, swap(): lax.all_to_all(values, axes, split_axis=0, concat_axis=0, tiled=False)  33.3 us
    all_gather x1, blocking collectives, body(): hidden = lax.all_gather(hidden, 'zh', axis=0, tiled=True)  24.7 us
    all_to_all x6, waiting for transfers between devices, swap(): lax.all_to_all(values, axes, split_axis=0, concat_axis=0, tiled=False)  22.9 us
    all_gather x1, blocking collectives, body(): ctx = lax.all_gather(context.T, 'zh', axis=0, tiled=False)  19.6 us
    ppermute x4, waiting for transfers between devices, shift_far(): return lax.ppermute(values, ('zh', 'c'), pairs)  19.4 us
    ppermute x4, starting transfers between devices, shift(): lax.ppermute(values, axis, [(i, (i + step) % count) for i in range(count)])  18.7 us
    all_gather x1, blocking collectives, body(): lax.all_gather(ctx, NEAR, axis=1, tiled=False).reshape(heads, token_count)  18.6 us
    ppermute x4, starting transfers between devices, shift_far(): return lax.ppermute(values, ('zh', 'c'), pairs)  17.9 us
  transfers between devices with their start and end apart: 14, of which 6 were waited for; matrix products, arithmetic and copies ran while one was open for 7% of the time, Pallas kernels for 0%

profile of v4, /device:TPU:1, one launch (start us, length us, event | category | flops | bytes accessed | tf_op | source)
XLA Modules:
  0.0 222.7 jit_solution(15506780922812414204)
XLA Ops:
  6.1 8.8 %collective-permute-start = (bf16[4,1408,128]{2,1,0:T(8,128)(2,1)}, bf16[4,1408,128]{2,1,0:T(8,128)(2,1)S(1)}, u32[]{:S(2)}, u32[]{:S(2)}) collective-permute-start(bf16[4,1408,128]{2,1,0:T(8,128)(2,1)} %get-tuple-element.42), channel_id=1, source_target_pairs={{0,1},{1,0},{2,3},{3,2},{4,5},{5,4},{6,7},{7,6},{8,9},{9,8},{10,11... | collective-permute-start | bytes 4325384 | tf_op jit(solution)/shard_map/ppermute | solution.py:27
  14.9 3.6 %all-to-all-start = ((bf16[16,128,128]{2,1,0:T(8,128)(2,1)}), bf16[16,128,128]{2,1,0:T(8,128)(2,1)S(1)}, u32[]{:S(2)}, u32[]{:S(2)}) async-start(bf16[16,128,128]{2,1,0:T(8,128)(2,1)} %bitcast.117), calls=%async_computation | async-start | bytes 1048576 | tf_op jit(solution)/shard_map/all_to_all | solution.py:15
  20.2 2.7 %fusion.6 = (bf16[1,2,1408,128]{3,2,1,0:T(8,128)(2,1)}, bf16[2,1408,128]{2,1,0:T(8,128)(2,1)S(1)}, bf16[2,1408,128]{2,1,0:T(8,128)(2,1)S(1)}, bf16[2,1408,128]{2,1,0:T(8,128)(2,1)}) fusion(s32[]{:T(128)S(6)} %select_n.148, bf16[4,1,1408,128]{3,2,1,0:T(8,128)(2,1)} %get-tuple-element.43, bf16[4,1,1408,128]{3,2,1,0:T(8,128)(2,1)S(1)} %bitcast.113, ...), kind=kLoop, calls=%fused_computation.30 | loop fusion | flops 1441792 | bytes 5767184 | tf_op jit(solution)/shard_map/stack | solution.py:41
  22.9 2.5 %collective-permute-start.1 = (bf16[2,1408,128]{2,1,0:T(8,128)(2,1)S(1)}, bf16[2,1408,128]{2,1,0:T(8,128)(2,1)S(1)}, u32[]{:S(2)}, u32[]{:S(2)}) collective-permute-start(bf16[2,1408,128]{2,1,0:T(8,128)(2,1)S(1)} %get-tuple-element.39), channel_id=1, source_target_pairs={{0,2},{2,4},{4,6},{6,0},{1,3},{3,5},{5,7},{7,1},{8,10},{10,12},{12... | collective-permute-start | bytes 2162696 | tf_op jit(solution)/shard_map/ppermute | solution.py:27
  25.5 4.0 %collective-permute-start.2 = (bf16[2,1408,128]{2,1,0:T(8,128)(2,1)S(1)}, bf16[2,1408,128]{2,1,0:T(8,128)(2,1)S(1)}, u32[]{:S(2)}, u32[]{:S(2)}) collective-permute-start(bf16[2,1408,128]{2,1,0:T(8,128)(2,1)S(1)} %get-tuple-element.40), channel_id=1, source_target_pairs={{0,6},{2,0},{4,2},{6,4},{1,7},{3,1},{5,3},{7,5},{8,14},{10,8},{12,... | collective-permute-start | bytes 2162696 | tf_op jit(solution)/shard_map/ppermute | solution.py:27
  29.4 19.6 %all-gather = bf16[256,128]{1,0:T(8,128)(2,1)S(1)} all-gather(bf16[64,128]{1,0:T(8,128)(2,1)S(1)} %bitcast.125), channel_id=2, replica_groups=mesh['zl'=4,'y'=4,'zh'=4,'x'=4,'c'=2] {'zh'}, dimensions={0}, use_global_device_ids=true | all-gather | bytes 81920 | tf_op jit(solution)/shard_map/all_gather | solution.py:112
  49.1 3.4 %collective-permute-start.3 = (bf16[2,1408,128]{2,1,0:T(8,128)(2,1)}, bf16[2,1408,128]{2,1,0:T(8,128)(2,1)}, u32[]{:S(2)}, u32[]{:S(2)}) collective-permute-start(bf16[2,1408,128]{2,1,0:T(8,128)(2,1)} %get-tuple-element.41), channel_id=1, source_target_pairs={{0,4},{2,6},{4,0},{6,2},{1,5},{3,7},{5,1},{7,3},{8,12},{10,14},{12... | collective-permute-start | bytes 2162696 | tf_op jit(solution)/shard_map/ppermute | solution.py:27
  53.7 7.0 %all-to-all-start.1 = ((bf16[16,128,128]{2,1,0:T(8,128)(2,1)}), bf16[16,128,128]{2,1,0:T(8,128)(2,1)S(1)}, u32[]{:S(2)}, u32[]{:S(2)}) async-start(bf16[16,128,128]{2,1,0:T(8,128)(2,1)} %broadcast_in_dim.19), calls=%async_computation.1 | async-start | bytes 1048576 | tf_op jit(solution)/shard_map/all_to_all | solution.py:15
  62.2 18.6 %all-gather.1 = bf16[4,512,128]{2,1,0:T(8,128)(2,1)} all-gather(bf16[4,64,128]{2,1,0:T(8,128)(2,1)S(1)} %bitcast.121), channel_id=3, replica_groups=mesh['zl'=4,'y'=4,'zh'=4,'x'=4,'c'=2] {'x','c'}, dimensions={1}, use_global_device_ids=true | all-gather | bytes 589824 | tf_op jit(solution)/shard_map/all_gather | solution.py:117
  84.7 7.2 %all-to-all-start.2 = ((bf16[16,25,128]{2,1,0:T(8,128)(2,1)}), bf16[16,25,128]{2,1,0:T(8,128)(2,1)S(1)}, u32[]{:S(2)}, u32[]{:S(2)}) async-start(bf16[16,25,128]{2,1,0:T(8,128)(2,1)} %fusion.34), calls=%async_computation.2 | async-start | bytes 262144 | tf_op jit(solution)/shard_map/all_to_all | solution.py:15
  96.1 3.8 %all-to-all-done.2 = bf16[16,25,128]{2,1,0:T(8,128)(2,1)S(1)} async-done(((bf16[16,25,128]{2,1,0:T(8,128)(2,1)}), bf16[16,25,128]{2,1,0:T(8,128)(2,1)S(1)}, u32[]{:S(2)}, u32[]{:S(2)}) %all-to-all-start.2) | async-done | bytes 102432 | tf_op jit(solution)/shard_map/all_to_all | solution.py:15
  100.0 15.0 %all-gather.2 = bf16[3200,128]{1,0:T(8,128)(2,1)S(1)} all-gather(bf16[400,128]{1,0:T(8,128)(2,1)S(1)} %pad_maximum_fusion.2), channel_id=4, replica_groups=mesh['zl'=4,'y'=4,'zh'=4,'x'=4,'c'=2] {'x','c'}, dimensions={0}, use_global_device_ids=true | all-gather | bytes 921600 | tf_op jit(solution)/shard_map/all_gather | solution.py:140
  117.0 4.0 %collective-permute-start.6 = (bf16[176,384]{1,0:T(8,128)(2,1)S(1)}, bf16[176,384]{1,0:T(8,128)(2,1)S(1)}, u32[]{:S(2)}, u32[]{:S(2)}) collective-permute-start(bf16[176,384]{1,0:T(8,128)(2,1)S(1)} %get-tuple-element.48), channel_id=1, source_target_pairs={{0,8},{1,25},{8,16},{9,1},{16,24},{17,9},{24,0},{25,17},{2,10},{3,... | collective-permute-start | bytes 405512 | tf_op jit(solution)/shard_map/ppermute | solution.py:61
  121.8 5.2 %collective-permute-start.4 = (bf16[184,384]{1,0:T(8,128)(2,1)S(1)}, bf16[184,384]{1,0:T(8,128)(2,1)}, u32[]{:S(2)}, u32[]{:S(2)}) collective-permute-start(bf16[184,384]{1,0:T(8,128)(2,1)S(1)} %get-tuple-element.47), channel_id=1, source_target_pairs={{0,24},{1,9},{8,0},{9,17},{16,8},{17,25},{24,16},{25,1},{2,26},{3,... | collective-permute-start | bytes 423944 | tf_op jit(solution)/shard_map/ppermute | solution.py:61
  127.0 4.2 %all-to-all-start.3 = ((bf16[8,704,128]{2,1,0:T(8,128)(2,1)}), bf16[8,704,128]{2,1,0:T(8,128)(2,1)S(1)}, u32[]{:S(2)}, u32[]{:S(2)}) async-start(bf16[8,704,128]{2,1,0:T(8,128)(2,1)} %bitcast.112), calls=%async_computation.3 | async-start | bytes 2883584 | tf_op jit(solution)/shard_map/all_to_all | solution.py:15
  131.3 4.0 %collective-permute-start.7 = (bf16[360,384]{1,0:T(8,128)(2,1)S(1)}, bf16[360,384]{1,0:T(8,128)(2,1)}, u32[]{:S(2)}, u32[]{:S(2)}) collective-permute-start(bf16[360,384]{1,0:T(8,128)(2,1)S(1)} %pad_maximum_fusion.1), channel_id=1, source_target_pairs={{0,8},{1,25},{8,16},{9,1},{16,24},{17,9},{24,0},{25,17},{2,10},{3,... | collective-permute-start | bytes 829448 | tf_op jit(solution)/shard_map/ppermute | solution.py:61
  138.3 4.7 %collective-permute-start.5 = (bf16[360,384]{1,0:T(8,128)(2,1)}, bf16[360,384]{1,0:T(8,128)(2,1)}, u32[]{:S(2)}, u32[]{:S(2)}) collective-permute-start(bf16[360,384]{1,0:T(8,128)(2,1)} %pad_maximum_fusion), channel_id=1, source_target_pairs={{0,24},{1,9},{8,0},{9,17},{16,8},{17,25},{24,16},{25,1},{2,26},{3,... | collective-permute-start | bytes 829448 | tf_op jit(solution)/shard_map/ppermute | solution.py:61
  143.0 14.3 %collective-permute-done.7 = bf16[360,384]{1,0:T(8,128)(2,1)} collective-permute-done((bf16[360,384]{1,0:T(8,128)(2,1)S(1)}, bf16[360,384]{1,0:T(8,128)(2,1)}, u32[]{:S(2)}, u32[]{:S(2)}) %collective-permute-start.7) | collective-permute-done | bytes 276512 | tf_op jit(solution)/shard_map/ppermute | solution.py:61
  157.3 3.9 %collective-permute-done.5 = bf16[360,384]{1,0:T(8,128)(2,1)} collective-permute-done((bf16[360,384]{1,0:T(8,128)(2,1)}, bf16[360,384]{1,0:T(8,128)(2,1)}, u32[]{:S(2)}, u32[]{:S(2)}) %collective-permute-start.5) | collective-permute-done | bytes 276512 | tf_op jit(solution)/shard_map/ppermute | solution.py:61
  163.4 24.7 %all_gather.27 = bf16[704,384]{1,0:T(8,128)(2,1)S(1)} all-gather(bf16[176,384]{1,0:T(8,128)(2,1)S(1)} %fusion.20), channel_id=1, replica_groups=mesh['zl'=4,'y'=4,'zh'=4,'x'=4,'c'=2] {'zh'}, dimensions={0}, use_global_device_ids=true | all-gather | bytes 675840 | tf_op jit(solution)/shard_map/all_gather | solution.py:162
  189.8 6.0 %all-to-all-start.4 = ((bf16[8,384,128]{2,1,0:T(8,128)(2,1)}), bf16[8,384,128]{2,1,0:T(8,128)(2,1)S(1)}, u32[]{:S(2)}, u32[]{:S(2)}) async-start(bf16[8,384,128]{2,1,0:T(8,128)(2,1)} %fusion.4), calls=%async_computation.4 | async-start | bytes 1572864 | tf_op jit(solution)/shard_map/all_to_all | solution.py:15
  195.9 12.2 %all-to-all-done.4 = bf16[8,384,128]{2,1,0:T(8,128)(2,1)S(1)} async-done(((bf16[8,384,128]{2,1,0:T(8,128)(2,1)}), bf16[8,384,128]{2,1,0:T(8,128)(2,1)S(1)}, u32[]{:S(2)}, u32[]{:S(2)}) %all-to-all-start.4) | async-done | bytes 786464 | tf_op jit(solution)/shard_map/all_to_all | solution.py:15
  208.9 5.3 %all-to-all-start.5 = ((bf16[16,24,128]{2,1,0:T(8,128)(2,1)}), bf16[16,24,128]{2,1,0:T(8,128)(2,1)S(1)}, u32[]{:S(2)}, u32[]{:S(2)}) async-start(bf16[16,24,128]{2,1,0:T(8,128)(2,1)} %multiply_convert_fusion), calls=%async_computation.5 | async-start | bytes 196608 | tf_op jit(solution)/shard_map/all_to_all | solution.py:15
  214.9 6.9 %all-to-all-done.5 = bf16[16,24,128]{2,1,0:T(8,128)(2,1)S(1)} async-done(((bf16[16,24,128]{2,1,0:T(8,128)(2,1)}), bf16[16,24,128]{2,1,0:T(8,128)(2,1)S(1)}, u32[]{:S(2)}, u32[]{:S(2)}) %all-to-all-start.5) | async-done | bytes 98336 | tf_op jit(solution)/shard_map/all_to_all | solution.py:15
  (102 shorter events, 29.7 us)
Async XLA Ops:
  0.6 82.3 %copy-start = (bf16[128,16]{0,1:T(8,128)(2,1)S(1)}, bf16[128,16]{0,1:T(8,128)(2,1)}, u32[]{:S(2)}) copy-start(bf16[128,16]{0,1:T(8,128)(2,1)} %param.13) | copy-start | bytes 12292
  4.3 14.3 %copy-start.6 = (bf16[128,128]{1,0:T(8,128)(2,1)S(1)}, bf16[128,128]{1,0:T(8,128)(2,1)}, u32[]{:S(2)}) copy-start(bf16[128,128]{1,0:T(8,128)(2,1)} %param.9) | copy-start | bytes 98308
  4.3 15.1 %copy-start.9 = (bf16[128]{0:T(256)(128)(2,1)S(1)}, bf16[128]{0:T(256)(128)(2,1)}, u32[]{:S(2)}) copy-start(bf16[128]{0:T(256)(128)(2,1)} %param.12) | copy-start | bytes 772
  4.4 15.1 %copy-start.8 = (s32[128,2]{0,1:T(2,128)S(1)}, s32[128,2]{0,1:T(2,128)}, u32[]{:S(2)}) copy-start(s32[128,2]{0,1:T(2,128)} %param.14) | copy-start | bytes 3076
  6.1 14.1 %collective-permute-start = (bf16[4,1408,128]{2,1,0:T(8,128)(2,1)}, bf16[4,1408,128]{2,1,0:T(8,128)(2,1)S(1)}, u32[]{:S(2)}, u32[]{:S(2)}) collective-permute-start(bf16[4,1408,128]{2,1,0:T(8,128)(2,1)} %get-tuple-element.42), channel_id=1, source_target_pairs={{0,1},{1,0},{2,3},{3,2},{4,5},{5,4},{6,7},{7,6},{8,9},{9,8},{10,11... | collective-permute-start | bytes 4325384 | tf_op jit(solution)/shard_map/ppermute | solution.py:27
  14.9 37.6 %all-to-all-start = ((bf16[16,128,128]{2,1,0:T(8,128)(2,1)}), bf16[16,128,128]{2,1,0:T(8,128)(2,1)S(1)}, u32[]{:S(2)}, u32[]{:S(2)}) async-start(bf16[16,128,128]{2,1,0:T(8,128)(2,1)} %bitcast.117), calls=%async_computation | async-start | bytes 1048576 | tf_op jit(solution)/shard_map/all_to_all | solution.py:15
  20.2 9.2 %copy-start.7 = (bf16[128,64]{0,1:T(8,128)(2,1)S(1)}, bf16[128,64]{0,1:T(8,128)(2,1)}, u32[]{:S(2)}) copy-start(bf16[128,64]{0,1:T(8,128)(2,1)} %param.10) | copy-start | bytes 49156
  22.9 29.7 %collective-permute-start.1 = (bf16[2,1408,128]{2,1,0:T(8,128)(2,1)S(1)}, bf16[2,1408,128]{2,1,0:T(8,128)(2,1)S(1)}, u32[]{:S(2)}, u32[]{:S(2)}) collective-permute-start(bf16[2,1408,128]{2,1,0:T(8,128)(2,1)S(1)} %get-tuple-element.39), channel_id=1, source_target_pairs={{0,2},{2,4},{4,6},{6,0},{1,3},{3,5},{5,7},{7,1},{8,10},{10,12},{12... | collective-permute-start | bytes 2162696 | tf_op jit(solution)/shard_map/ppermute | solution.py:27
  25.5 27.2 %collective-permute-start.2 = (bf16[2,1408,128]{2,1,0:T(8,128)(2,1)S(1)}, bf16[2,1408,128]{2,1,0:T(8,128)(2,1)S(1)}, u32[]{:S(2)}, u32[]{:S(2)}) collective-permute-start(bf16[2,1408,128]{2,1,0:T(8,128)(2,1)S(1)} %get-tuple-element.40), channel_id=1, source_target_pairs={{0,6},{2,0},{4,2},{6,4},{1,7},{3,1},{5,3},{7,5},{8,14},{10,8},{12,... | collective-permute-start | bytes 2162696 | tf_op jit(solution)/shard_map/ppermute | solution.py:27
  49.1 31.7 %collective-permute-start.3 = (bf16[2,1408,128]{2,1,0:T(8,128)(2,1)}, bf16[2,1408,128]{2,1,0:T(8,128)(2,1)}, u32[]{:S(2)}, u32[]{:S(2)}) collective-permute-start(bf16[2,1408,128]{2,1,0:T(8,128)(2,1)} %get-tuple-element.41), channel_id=1, source_target_pairs={{0,4},{2,6},{4,0},{6,2},{1,5},{3,7},{5,1},{7,3},{8,12},{10,14},{12... | collective-permute-start | bytes 2162696 | tf_op jit(solution)/shard_map/ppermute | solution.py:27
  52.7 8.1 %copy-start.3 = (bf16[2,1408,128]{2,1,0:T(8,128)(2,1)}, bf16[2,1408,128]{2,1,0:T(8,128)(2,1)S(1)}, u32[]{:S(2)}) copy-start(bf16[2,1408,128]{2,1,0:T(8,128)(2,1)S(1)} %collective-permute-done.1) | copy-start | bytes 2162692
  52.7 8.1 %copy-start.2 = (bf16[2,1408,128]{2,1,0:T(8,128)(2,1)}, bf16[2,1408,128]{2,1,0:T(8,128)(2,1)S(1)}, u32[]{:S(2)}) copy-start(bf16[2,1408,128]{2,1,0:T(8,128)(2,1)S(1)} %collective-permute-done.2) | copy-start | bytes 2162692
  53.7 27.1 %all-to-all-start.1 = ((bf16[16,128,128]{2,1,0:T(8,128)(2,1)}), bf16[16,128,128]{2,1,0:T(8,128)(2,1)S(1)}, u32[]{:S(2)}, u32[]{:S(2)}) async-start(bf16[16,128,128]{2,1,0:T(8,128)(2,1)} %broadcast_in_dim.19), calls=%async_computation.1 | async-start | bytes 1048576 | tf_op jit(solution)/shard_map/all_to_all | solution.py:15
  60.8 1.1 copy-start.1
  60.8 1.3 copy-start.4
  84.7 15.2 %all-to-all-start.2 = ((bf16[16,25,128]{2,1,0:T(8,128)(2,1)}), bf16[16,25,128]{2,1,0:T(8,128)(2,1)S(1)}, u32[]{:S(2)}, u32[]{:S(2)}) async-start(bf16[16,25,128]{2,1,0:T(8,128)(2,1)} %fusion.34), calls=%async_computation.2 | async-start | bytes 262144 | tf_op jit(solution)/shard_map/all_to_all | solution.py:15
  117.0 14.2 %collective-permute-start.6 = (bf16[176,384]{1,0:T(8,128)(2,1)S(1)}, bf16[176,384]{1,0:T(8,128)(2,1)S(1)}, u32[]{:S(2)}, u32[]{:S(2)}) collective-permute-start(bf16[176,384]{1,0:T(8,128)(2,1)S(1)} %get-tuple-element.48), channel_id=1, source_target_pairs={{0,8},{1,25},{8,16},{9,1},{16,24},{17,9},{24,0},{25,17},{2,10},{3,... | collective-permute-start | bytes 405512 | tf_op jit(solution)/shard_map/ppermute | solution.py:61
  121.8 14.8 %collective-permute-start.4 = (bf16[184,384]{1,0:T(8,128)(2,1)S(1)}, bf16[184,384]{1,0:T(8,128)(2,1)}, u32[]{:S(2)}, u32[]{:S(2)}) collective-permute-start(bf16[184,384]{1,0:T(8,128)(2,1)S(1)} %get-tuple-element.47), channel_id=1, source_target_pairs={{0,24},{1,9},{8,0},{9,17},{16,8},{17,25},{24,16},{25,1},{2,26},{3,... | collective-permute-start | bytes 423944 | tf_op jit(solution)/shard_map/ppermute | solution.py:61
  127.0 61.1 %all-to-all-start.3 = ((bf16[8,704,128]{2,1,0:T(8,128)(2,1)}), bf16[8,704,128]{2,1,0:T(8,128)(2,1)S(1)}, u32[]{:S(2)}, u32[]{:S(2)}) async-start(bf16[8,704,128]{2,1,0:T(8,128)(2,1)} %bitcast.112), calls=%async_computation.3 | async-start | bytes 2883584 | tf_op jit(solution)/shard_map/all_to_all | solution.py:15
  131.3 26.0 %collective-permute-start.7 = (bf16[360,384]{1,0:T(8,128)(2,1)S(1)}, bf16[360,384]{1,0:T(8,128)(2,1)}, u32[]{:S(2)}, u32[]{:S(2)}) collective-permute-start(bf16[360,384]{1,0:T(8,128)(2,1)S(1)} %pad_maximum_fusion.1), channel_id=1, source_target_pairs={{0,8},{1,25},{8,16},{9,1},{16,24},{17,9},{24,0},{25,17},{2,10},{3,... | collective-permute-start | bytes 829448 | tf_op jit(solution)/shard_map/ppermute | solution.py:61
  138.3 22.9 %collective-permute-start.5 = (bf16[360,384]{1,0:T(8,128)(2,1)}, bf16[360,384]{1,0:T(8,128)(2,1)}, u32[]{:S(2)}, u32[]{:S(2)}) collective-permute-start(bf16[360,384]{1,0:T(8,128)(2,1)} %pad_maximum_fusion), channel_id=1, source_target_pairs={{0,24},{1,9},{8,0},{9,17},{16,8},{17,25},{24,16},{25,1},{2,26},{3,... | collective-permute-start | bytes 829448 | tf_op jit(solution)/shard_map/ppermute | solution.py:61
  189.8 24.4 %copy-start.5 = (bf16[128,128]{0,1:T(8,128)(2,1)S(1)}, bf16[128,128]{0,1:T(8,128)(2,1)}, u32[]{:S(2)}) copy-start(bf16[128,128]{0,1:T(8,128)(2,1)} %get-tuple-element.51) | copy-start | bytes 98308
  189.8 18.3 %all-to-all-start.4 = ((bf16[8,384,128]{2,1,0:T(8,128)(2,1)}), bf16[8,384,128]{2,1,0:T(8,128)(2,1)S(1)}, u32[]{:S(2)}, u32[]{:S(2)}) async-start(bf16[8,384,128]{2,1,0:T(8,128)(2,1)} %fusion.4), calls=%async_computation.4 | async-start | bytes 1572864 | tf_op jit(solution)/shard_map/all_to_all | solution.py:15
  208.9 12.9 %all-to-all-start.5 = ((bf16[16,24,128]{2,1,0:T(8,128)(2,1)}), bf16[16,24,128]{2,1,0:T(8,128)(2,1)S(1)}, u32[]{:S(2)}, u32[]{:S(2)}) async-start(bf16[16,24,128]{2,1,0:T(8,128)(2,1)} %multiply_convert_fusion), calls=%async_computation.5 | async-start | bytes 196608 | tf_op jit(solution)/shard_map/all_to_all | solution.py:15
